TPU v7x, 32 devices: a whole 2x2x4 slice. The times are simulated.
32 devices in a mesh: dp: 8 (over y, x, core), tensor: 2 (over z_hi), seq: 2 (over z_lo).
Axes of the slice: x: 2, y: 2, z: 4 (z_hi: 2, z_lo: 2; z = z_hi * 2 + z_lo), core: 2. Of those that a mesh axis runs over, the one named last changes fastest.
Arguments:
- frames: bfloat16 [8, 1500, 768], P('dp', 'seq'), may hold values from -6 to 6
- languages: int32 [8], P('dp'), may hold values from 0 to 98
- present: int32 [8], P('dp'), may hold values 0 or 1
- lang_table: bfloat16 [99, 768], replicated, may hold values from -3 to 3
- norm1_gain: bfloat16 [768], replicated, may hold values from 0.099609375 to 1.8984375
- norm1_shift: bfloat16 [768], replicated, may hold values from -2 to 2
- qkv_weight: bfloat16 [3, 768, 768], P(None, None, 'tensor'), may hold values from -0.3125 to 0.3125
- qkv_bias: bfloat16 [2, 768], P(None, 'tensor'), may hold values from -2 to 2
- out_weight: bfloat16 [768, 768], P('tensor'), may hold values from -0.625 to 0.625
- out_bias: bfloat16 [768], replicated, may hold values from -2 to 2
- norm2_gain: bfloat16 [768], replicated, may hold values from 0.099609375 to 1.8984375
- norm2_shift: bfloat16 [768], replicated, may hold values from -2 to 2
- up_weight: bfloat16 [768, 3072], P(None, 'tensor'), may hold values from -0.21875 to 0.21875
- up_bias: bfloat16 [3072], P('tensor'), may hold values from -3 to 3
- down_weight: bfloat16 [3072, 768], P('tensor'), may hold values from -0.15625 to 0.15625
- down_bias: bfloat16 [768], replicated, may hold values from -2 to 2
- grad_out: bfloat16 [8, 1500, 768], P('dp', 'seq'), may hold values from -6 to 6
Outputs:
- output: bfloat16 [8, 1500, 768], P('dp', 'seq')
- grad_frames: bfloat16 [8, 1500, 768], P('dp', 'seq')
- grad_lang_table: float32 [99, 768], replicated
- grad_norm1_gain: float32 [768], replicated
- grad_norm1_shift: float32 [768], replicated
- grad_qkv_weight: float32 [3, 768, 768], P(None, None, 'tensor')
- grad_qkv_bias: float32 [2, 768], P(None, 'tensor')
- grad_out_weight: float32 [768, 768], P('tensor')
- grad_out_bias: float32 [768], replicated
- grad_norm2_gain: float32 [768], replicated
- grad_norm2_shift: float32 [768], replicated
- grad_up_weight: float32 [768, 3072], P(None, 'tensor')
- grad_up_bias: float32 [3072], P('tensor')
- grad_down_weight: float32 [3072, 768], P('tensor')
- grad_down_bias: float32 [768], replicated
Inputs may be any that keep to these rules, and one draw needn't show every extreme that they name: `languages`: a language group per clip slot, of 99. `present`: padded slots carry 0.
All inputs are finite; a program needn't handle non-finite values. No bound on the sum of `present` on one device may be relied on, other than what follows from the above.
Results may differ from a plain program's by a relative error of at most 0.013.
The roundings to bfloat16 on the way count: a program that leaves them out, or rounds other values in their place, can miss the bound.
Values may be sent and summed in bfloat16 or wider, within the bound.
A program may use at most 256 MiB of HBM per device.

v0:
```python
import jax
import jax.numpy as jnp
from jax import lax
from jax.sharding import PartitionSpec as P

HEAD = 64


epsilon = 1e-05
query_scale = 0.125


def layer_norm(inputs, scales, shifts):
    row_mean = jnp.mean(inputs, axis=-1, keepdims=True)
    centred = inputs - row_mean
    variance = jnp.mean(centred * centred, axis=-1, keepdims=True)
    return centred * lax.rsqrt(variance + epsilon) * scales + shifts


def exact_gelu(inputs):
    return jax.nn.gelu(inputs, approximate=False)


def attend(operands):
    queries, key_rows, values = operands
    scores = jnp.einsum("qhd,khd->hqk", queries, key_rows, preferred_element_type=jnp.float32)
    row_max = jnp.max(scores, axis=-1, keepdims=True)
    weights = jnp.exp(scores - row_max)
    row_total = jnp.sum(weights, axis=-1, keepdims=True)
    weights = weights / row_total
    mixed_heads = jnp.einsum(
        "hqk,khd->qhd", weights.astype(jnp.bfloat16), values, preferred_element_type=jnp.float32
    )
    return (mixed_heads, (row_max + jnp.log(row_total))[..., 0])


def attend_back(operands):
    queries, key_rows, values, log_total, grad_mixed = operands
    scores = jnp.einsum("qhd,khd->hqk", queries, key_rows, preferred_element_type=jnp.float32)
    weights = jnp.exp(scores - log_total[..., None])
    grad_weights = jnp.einsum(
        "qhd,khd->hqk", grad_mixed, values, preferred_element_type=jnp.float32
    )
    inner_sum = jnp.sum(grad_weights * weights, axis=-1, keepdims=True)
    grad_scores = (weights * (grad_weights - inner_sum)).astype(jnp.bfloat16)
    grad_queries = jnp.einsum(
        "hqk,khd->qhd", grad_scores, key_rows, preferred_element_type=jnp.float32
    )
    grad_keys = jnp.einsum("hqk,qhd->khd", grad_scores, queries, preferred_element_type=jnp.float32)
    grad_values = jnp.einsum(
        "hqk,qhd->khd", weights.astype(jnp.bfloat16), grad_mixed, preferred_element_type=jnp.float32
    )
    return (grad_queries, grad_keys, grad_values)


def on_device(
    frames,
    languages,
    present,
    lang_table,
    norm1_gain,
    norm1_shift,
    qkv_weight,
    qkv_bias,
    out_weight,
    out_bias,
    norm2_gain,
    norm2_shift,
    up_weight,
    up_bias,
    down_weight,
    down_bias,
    grad_out,
):
    slot_count, local_frames, model_width = frames.shape
    local_width = qkv_weight.shape[2]
    local_heads = local_width // HEAD
    lang_count = lang_table.shape[0]
    gain_two = norm2_gain.astype(jnp.float32)
    shift_two = norm2_shift.astype(jnp.float32)
    keep_mask = present.astype(jnp.float32)[:, None, None]
    one_hot = (
        languages[:, None] == lax.broadcasted_iota(jnp.int32, (slot_count, lang_count), 1)
    ).astype(jnp.float32)
    embedding = jnp.dot(one_hot, lang_table.astype(jnp.float32), precision=lax.Precision.HIGHEST)
    stream = frames.astype(jnp.float32) + embedding[:, None, :]
    normed1, norm1_back = jax.vjp(
        layer_norm, stream, norm1_gain.astype(jnp.float32), norm1_shift.astype(jnp.float32)
    )
    normed1 = normed1.astype(jnp.bfloat16)
    projected = jnp.einsum("sfd,jde->jsfe", normed1, qkv_weight, preferred_element_type=jnp.float32)
    queries = ((projected[0] + qkv_bias[0].astype(jnp.float32)) * query_scale).astype(jnp.bfloat16)
    key_rows = projected[1].astype(jnp.bfloat16)
    values = (projected[2] + qkv_bias[1].astype(jnp.float32)).astype(jnp.bfloat16)
    all_keys, all_values = (
        lax.all_gather(key_rows, "seq", axis=1, tiled=True),
        lax.all_gather(values, "seq", axis=1, tiled=True),
    )
    total_frames = all_keys.shape[1]
    query_heads = queries.reshape(slot_count, local_frames, local_heads, HEAD)
    key_heads = all_keys.reshape(slot_count, total_frames, local_heads, HEAD)
    value_heads = all_values.reshape(slot_count, total_frames, local_heads, HEAD)
    mixed_heads, log_total = lax.map(attend, (query_heads, key_heads, value_heads))
    mixed_low = mixed_heads.reshape(slot_count, local_frames, local_width).astype(jnp.bfloat16)
    attention_part = jnp.einsum(
        "sfe,ed->sfd", mixed_low, out_weight, preferred_element_type=jnp.float32
    )
    attention = lax.psum(attention_part, "tensor")
    hidden1 = stream + attention + out_bias.astype(jnp.float32)
    normed2, norm2_back = jax.vjp(layer_norm, hidden1, gain_two, shift_two)
    normed2 = normed2.astype(jnp.bfloat16)
    pre_act = jnp.einsum(
        "sfd,dh->sfh", normed2, up_weight, preferred_element_type=jnp.float32
    ) + up_bias.astype(jnp.float32)
    activation, gelu_back = jax.vjp(exact_gelu, pre_act)
    activation = activation.astype(jnp.bfloat16)
    feed_part = jnp.einsum(
        "sfh,hd->sfd", activation, down_weight, preferred_element_type=jnp.float32
    )
    feed = lax.psum(feed_part.astype(jnp.bfloat16), "tensor").astype(jnp.float32)
    output = (keep_mask * (hidden1 + feed + down_bias.astype(jnp.float32))).astype(jnp.bfloat16)
    grad_rows = keep_mask * grad_out.astype(jnp.float32)
    grad_low = grad_rows.astype(jnp.bfloat16)
    grad_down_bias = jnp.sum(grad_rows, axis=(0, 1))
    grad_down_weight = jnp.einsum(
        "sfh,sfd->hd", activation, grad_low, preferred_element_type=jnp.float32
    )
    grad_activation = jnp.einsum(
        "sfd,hd->sfh", grad_low, down_weight, preferred_element_type=jnp.float32
    )
    grad_pre = gelu_back(grad_activation)[0].astype(jnp.bfloat16)
    grad_up_bias = jnp.sum(grad_pre.astype(jnp.float32), axis=(0, 1))
    grad_up_weight = jnp.einsum(
        "sfd,sfh->dh", normed2, grad_pre, preferred_element_type=jnp.float32
    )
    norm2_part = jnp.einsum("sfh,dh->sfd", grad_pre, up_weight, preferred_element_type=jnp.float32)
    grad_normed2 = lax.psum(norm2_part, "tensor")
    grad_hidden_norm, grad_norm2_gain, grad_norm2_shift = norm2_back(grad_normed2)
    grad_hidden1 = grad_rows + grad_hidden_norm
    grad_out_bias = jnp.sum(grad_hidden1, axis=(0, 1))
    mlp_set = (
        grad_norm2_gain,
        grad_norm2_shift,
        grad_up_weight,
        grad_up_bias,
        grad_down_weight,
        grad_down_bias,
    )
    grad_attn_low = grad_hidden1.astype(jnp.bfloat16)
    grad_out_weight = jnp.einsum(
        "sfe,sfd->ed", mixed_low, grad_attn_low, preferred_element_type=jnp.float32
    )
    grad_mixed = jnp.einsum(
        "sfd,ed->sfe", grad_attn_low, out_weight, preferred_element_type=jnp.float32
    ).astype(jnp.bfloat16)
    grad_mixed_heads = grad_mixed.reshape(slot_count, local_frames, local_heads, HEAD)
    grad_query_heads, grad_key_heads, grad_value_heads = lax.map(
        attend_back, (query_heads, key_heads, value_heads, log_total, grad_mixed_heads)
    )
    grad_key_share, grad_value_share = (
        lax.psum_scatter(
            grad_key_heads.reshape(slot_count, total_frames, local_width),
            "seq",
            scatter_dimension=1,
            tiled=True,
        ),
        lax.psum_scatter(
            grad_value_heads.reshape(slot_count, total_frames, local_width),
            "seq",
            scatter_dimension=1,
            tiled=True,
        ),
    )
    grad_query_low = grad_query_heads.reshape(slot_count, local_frames, local_width).astype(
        jnp.bfloat16
    )
    grad_query_pre = (grad_query_low.astype(jnp.float32) * query_scale).astype(jnp.bfloat16)
    grad_value_low = grad_value_share.astype(jnp.bfloat16)
    stacked = jnp.stack([grad_query_pre, grad_key_share.astype(jnp.bfloat16), grad_value_low])
    grad_qkv_weight = jnp.einsum(
        "sfd,jsfe->jde", normed1, stacked, preferred_element_type=jnp.float32
    )
    grad_qkv_bias = jnp.stack(
        [
            jnp.sum(grad_query_pre.astype(jnp.float32), axis=(0, 1)),
            jnp.sum(grad_value_low.astype(jnp.float32), axis=(0, 1)),
        ]
    )
    norm1_part = jnp.einsum(
        "jsfe,jde->sfd", stacked, qkv_weight, preferred_element_type=jnp.float32
    )
    grad_normed1 = lax.psum(norm1_part, "tensor")
    grad_stream_norm, grad_norm1_gain, grad_norm1_shift = norm1_back(grad_normed1)
    grad_stream = grad_hidden1 + grad_stream_norm
    grad_frames = grad_stream.astype(jnp.bfloat16)
    grad_lang_table = jnp.dot(
        one_hot.T, jnp.sum(grad_stream, axis=1), precision=lax.Precision.HIGHEST
    )
    attention_set = (
        grad_lang_table,
        grad_norm1_gain,
        grad_norm1_shift,
        grad_qkv_weight,
        grad_qkv_bias,
        grad_out_weight,
        grad_out_bias,
    )
    merged = lax.psum(attention_set + mlp_set, ("dp", "seq"))
    attention_set = merged[:7]
    mlp_set = merged[7:]
    return (
        output,
        grad_frames,
        attention_set[0],
        attention_set[1],
        attention_set[2],
        attention_set[3],
        attention_set[4],
        attention_set[5],
        attention_set[6],
        mlp_set[0],
        mlp_set[1],
        mlp_set[2],
        mlp_set[3],
        mlp_set[4],
        mlp_set[5],
    )


def solution(mesh):
    placed = (
        P("dp", "seq", None),
        P("dp"),
        P("dp"),
        P(),
        P(),
        P(),
        P(None, None, "tensor"),
        P(None, "tensor"),
        P("tensor", None),
        P(),
        P(),
        P(),
        P(None, "tensor"),
        P("tensor"),
        P("tensor", None),
        P(),
        P("dp", "seq", None),
    )
    return jax.shard_map(
        on_device,
        mesh=mesh,
        in_specs=placed,
        out_specs=(
            P("dp", "seq", None),
            P("dp", "seq", None),
            P(),
            P(),
            P(),
            P(None, None, "tensor"),
            P(None, "tensor"),
            P("tensor", None),
            P(),
            P(),
            P(),
            P(None, "tensor"),
            P("tensor"),
            P("tensor", None),
            P(),
        ),
        check_vma=False,
    )
```

profile of v0, /device:TPU:0, one launch (start us, length us, event | category | flops | bytes accessed | tf_op | source)
XLA Modules:
  0.0 2151.5 jit_solution(15486912216630569080)
XLA Ops:
  30.2 29.6 %all-gather.6.cloned.1.call-done = bf16[1,1,1500,384]{3,1,0,2:T(2,128)(2,1)} async-done(((bf16[1,1,750,384]{3,1,0,2:T(2,128)(2,1)}), bf16[1,1,1500,384]{3,1,0,2:T(2,128)(2,1)}) %all-gather.6.cloned.1.call-update) | async-done | bytes 1152016 | tf_op jit(solution)/shard_map/all_gather | solution.py:96
  59.8 6.4 copy.55
  66.3 14.7 fusion.65
  81.0 11.7 fusion
  97.4 6.4 copy.52
  103.9 11.9 fusion.21
  122.5 114.9 %all-reduce.12.cloned.1.call-done = f32[1,750,768]{2,1,0:T(8,128)} async-done(((f32[1,750,768]{2,1,0:T(8,128)}), f32[1,750,768]{2,1,0:T(8,128)}) %all-reduce.12.cloned.1.call-update) | async-done | bytes 2304016 | tf_op jit(solution)/shard_map/psum | solution.py:108
  241.0 12.7 multiply_convert_fusion.1
  262.9 5.5 fusion.17
  270.3 110.1 %all-reduce.16.cloned.1.call-done = f32[1,750,768]{2,1,0:T(8,128)} async-done(((f32[1,750,768]{2,1,0:T(8,128)}), f32[1,750,768]{2,1,0:T(8,128)}) %all-reduce.16.cloned.1.call-update) | async-done | bytes 2304016 | tf_op jit(solution)/shard_map/psum | solution.py:137
  383.0 67.5 %all-reduce.14.cloned.1.call-done = bf16[1,750,768]{2,1,0:T(8,128)(2,1)} async-done(((bf16[1,750,768]{2,1,0:T(8,128)(2,1)}), bf16[1,750,768]{2,1,0:T(8,128)(2,1)}) %all-reduce.14.cloned.1.call-update) | async-done | bytes 1152016 | tf_op jit(solution)/shard_map/psum | solution.py:120
  460.2 17.8 multiply_reduce_fusion
  478.0 14.9 fusion.2
  492.9 22.6 %multiply_convert_fusion = bf16[6,750,1500]{2,1,0:T(8,128)(2,1)} fusion(f32[6,750,1500]{2,1,0:T(8,128)} %get-tuple-element.146, f32[6,750,1500]{2,1,0:T(8,128)} %get-tuple-element.143, f32[6,750]{1,0:T(8,128)S(1)} %get-tuple-element.145, f32[6,750]{1,0:T(8,128)S(1)} %log_add_fusion), kind=kLoop, calls=%fused_computation | loop fusion | flops 27000000 | bytes 67536000 | tf_op jit(solution)/shard_map/while/body/eval_jaxpr/convert_element_type | solution.py:45
  515.6 9.4 fusion.42
  524.9 9.9 convert_reduce_fusion.1
  534.8 6.6 copy.57
  541.4 6.6 copy.59
  548.0 831.9 %all-reduce.21 = (bf16[1,1500,384]{2,0,1:T(2,128)(2,1)}, bf16[1,1500,384]{2,0,1:T(2,128)(2,1)}) all-reduce(f32[1,1500,384]{2,0,1:T(1,128)} %copy.59, f32[1,1500,384]{2,0,1:T(1,128)} %copy.57), channel_id=4, replica_groups=mesh['dp'=8,'tensor'=2,'seq'=2] {'seq'}, use_global_device_ids=true, to_apply=%region_13.14.clone | all-reduce | flops 1152000 | bytes 6912000
  1393.6 6.3 fusion.30
  1409.9 102.4 %all-reduce.18.cloned.1.call-done = f32[1,750,768]{2,1,0:T(8,128)} async-done(((f32[1,750,768]{2,1,0:T(8,128)}), f32[1,750,768]{2,1,0:T(8,128)}) %all-reduce.18.cloned.1.call-update) | async-done | bytes 2304016 | tf_op jit(solution)/shard_map/psum | solution.py:192
  1520.6 54.5 %all-reduce.2 = (f32[768]{0:T(1024)}, f32[768]{0:T(1024)}, f32[2,384]{1,0:T(2,128)}, f32[768]{0:T(1024)}, f32[768]{0:T(1024)}, /*index=5*/f32[768]{0:T(1024)}, f32[1536]{0:T(1024)}, f32[768]{0:T(1024)}) all-reduce(f32[768]{0:T(1024)S(1)} %get-tuple-element.107, ...), channel_id=1, replica_groups=mesh['dp'=8,'tensor'=2,'seq'=2] {'dp','seq'}, use_global_device_ids=true, to_apply=%region_20.21 | all-reduce | flops 6912 | bytes 55296 | tf_op jit(solution)/shard_map/psum | solution.py:208
  1575.0 553.3 %all-reduce.20.cloned.1.call-done = (f32[99,768]{1,0:T(8,128)}, f32[3,768,384]{1,2,0:T(8,128)}, f32[384,768]{1,0:T(8,128)}, f32[768,1536]{1,0:T(8,128)}, f32[1536,768]{1,0:T(8,128)}) async-done(((f32[99,768]{1,0:T(8,128)}, f32[3,768,384]{1,2,0:T(8,128)}, f32[384,768]{1,0:T(8,128)}, f32[768,1536]{1,0:T(8,128)}, f32[1536,768]{1,0:T(8,128)}), (f32[99,768]{1,0:T(8,128)}, f32[3,768,384]{1,2,0:T(8,128)}, ...) | async-done | bytes 14459920 | tf_op jit(solution)/shard_map/psum | solution.py:208
  2135.4 5.5 copy.90
  (192 shorter events, 100.9 us)
Async XLA Ops:
  7.2 233.8 %copy-start = (bf16[768,1536]{1,0:T(8,128)(2,1)S(1)}, bf16[768,1536]{1,0:T(8,128)(2,1)}, u32[]{:S(2)}) copy-start(bf16[768,1536]{1,0:T(8,128)(2,1)} %param.29) | copy-start | bytes 7077892
  7.2 7.1 copy-start.7
  7.2 52.6 %all-gather.6.cloned.1.call-start = ((), (), s32[]{:S(2)}) async-start(), calls=%async_computation.5 | async-start | bytes 3456000 | tf_op jit(solution)/shard_map/all_gather | solution.py:96
  21.5 75.9 %all-gather.4.cloned.1.call-start = ((), (), s32[]{:S(2)}) async-start(), calls=%async_computation | async-start | bytes 3456000 | tf_op jit(solution)/shard_map/all_gather | solution.py:97
  24.9 212.6 %all-reduce.12.cloned.1.call-start = ((), (), s32[]{:S(2)}) async-start(), calls=%async_computation.1 | async-start | bytes 4620288 | tf_op jit(solution)/shard_map/psum | solution.py:108
  30.2 50.8 %copy-start.23 = (f32[6,64]{1,0:T(8,128)}, f32[6,64]{1,0:T(8,128)S(1)}, u32[]{:S(2)}) copy-start(f32[6,64]{1,0:T(8,128)S(1)} %reshape.487) | copy-start | bytes 4612
  103.9 12.8 copy-start.13
  118.9 261.6 %all-reduce.16.cloned.1.call-start = ((), (), s32[]{:S(2)}) async-start(), calls=%async_computation.3 | async-start | bytes 4620288 | tf_op jit(solution)/shard_map/psum | solution.py:137
  239.6 14.1 copy-start.2
  241.0 209.5 %copy-start.29 = (f32[750]{0:T(1024)}, f32[750]{0:T(1024)S(1)}, u32[]{:S(2)}) copy-start(f32[750]{0:T(1024)S(1)} %fusion.45) | copy-start | bytes 9004
  241.0 12.7 copy-start.18
  241.0 12.7 copy-start.52
  262.8 187.7 %all-reduce.14.cloned.1.call-start = ((), (), s32[]{:S(2)}) async-start(), calls=%async_computation.2 | async-start | bytes 2310144 | tf_op jit(solution)/shard_map/psum | solution.py:120
  262.8 7.4 copy-start.26
  262.8 117.6 %copy-start.3 = (f32[1,750,768]{2,1,0:T(8,128)S(1)}, f32[1,750,768]{2,1,0:T(8,128)}, u32[]{:S(2)}) copy-start(f32[1,750,768]{2,1,0:T(8,128)} %copy-done.2) | copy-start | bytes 6912004
  268.4 1244.0 %all-reduce.18.cloned.1.call-start = ((), (), s32[]{:S(2)}) async-start(), calls=%async_computation.4 | async-start | bytes 4620288 | tf_op jit(solution)/shard_map/psum | solution.py:192
  270.3 112.7 %copy-start.34 = (f32[750]{0:T(1024)S(1)}, f32[750]{0:T(1024)}, u32[]{:S(2)}) copy-start(f32[750]{0:T(1024)} %copy-done.33) | copy-start | bytes 9004
  270.3 180.2 %copy-start.39 = (f32[768]{0:T(1024)S(1)}, f32[768]{0:T(1024)}, u32[]{:S(2)}) copy-start(f32[768]{0:T(1024)} %convert_element_type.240) | copy-start | bytes 9220
  492.9 22.6 %copy-start.24 = (f32[6,64]{1,0:T(8,128)S(1)}, f32[6,64]{1,0:T(8,128)}, u32[]{:S(2)}) copy-start(f32[6,64]{1,0:T(8,128)} %copy-done.23) | copy-start | bytes 4612
  515.6 9.4 copy-start.8
  1393.2 735.1 %all-reduce.20.cloned.1.call-start = ((), (), s32[]{:S(2)}) async-start(), calls=%async_computation.6 | async-start | bytes 28950528 | tf_op jit(solution)/shard_map/psum | solution.py:208
  1393.6 6.4 copy-start.30
  1409.9 105.2 %copy-start.32 = (f32[750]{0:T(1024)S(1)}, f32[750]{0:T(1024)}, u32[]{:S(2)}) copy-start(f32[750]{0:T(1024)} %copy-done.31) | copy-start | bytes 9004
  2134.3 6.5 slice-start
  (41 other events, 113.2 us)
Sparse Core Ops, SparseCore 0:
  21.6 38.1 all-gather.5
  62.0 35.4 all-gather.3
  119.0 118.4 all-reduce.11
  262.9 117.5 all-reduce.15
  383.2 67.1 all-reduce.13
  1393.4 118.9 all-reduce.17
  1519.2 609.0 all-reduce.19
where the time goes:
time: 2160 us; the launch traced here: 2150 us
  waiting for transfers between devices  983 us (46%)
  blocking collectives  886 us (41%)
  matrix products  134 us (6%)
  local copies, waits for them, and re-layouts  71.8 us (3%)
  other arithmetic  58.2 us (3%)
    unnamed x1, blocking collectives  832 us
    psum x1, waiting for transfers between devices, on_device(): merged = lax.psum(attention_set + mlp_set, ('dp', 'seq'))  553 us
    psum x1, waiting for transfers between devices, on_device(): attention = lax.psum(attention_part, 'tensor')  115 us
    psum x1, waiting for transfers between devices, on_device(): grad_normed2 = lax.psum(norm2_part, 'tensor')  110 us
    psum x1, waiting for transfers between devices, on_device(): grad_normed1 = lax.psum(norm1_part, 'tensor')  102 us
    psum x1, waiting for transfers between devices, on_device(): lax.psum(feed_part.astype(jnp.bfloat16), 'tensor').astype(jnp.float32)  67.5 us
    psum x1, blocking collectives, on_device(): merged = lax.psum(attention_set + mlp_set, ('dp', 'seq'))  54.5 us
  transfers between devices with their start and end apart: 7, of which 7 were waited for; matrix products, arithmetic and copies ran while one was open for 3% of the time, Pallas kernels for 0%

commit v1 on v0

v1 whole, which is shorter than its diff:
```python
import jax
import jax.numpy as jnp
from jax import lax
from jax.sharding import PartitionSpec as P

HEAD = 64
EPSILON = 1e-05
QUERY_SCALE = 0.125
AXES = ("dp", "tensor", "seq")
F32 = jnp.float32
BF16 = jnp.bfloat16


class Grid:
    def __init__(self, mesh):
        self.dp, self.tp, self.sp = (mesh.shape[name] for name in AXES)
        self.pairs = self.dp // 2

    def send(self, value, target):
        moves = []
        for d in range(self.dp):
            for t in range(self.tp):
                for s in range(self.sp):
                    to = target(d, t, s)
                    if to is not None:
                        moves.append((self.flat(d, t, s), self.flat(*to)))
        return lax.ppermute(value, AXES, moves)

    def flat(self, d, t, s):
        return (d * self.tp + t) * self.sp + s

    def levels(self):
        d, s = lax.axis_index("dp"), lax.axis_index("seq")
        steps = [(lambda d, t, s: (d, t, s ^ 1), s)]
        bit = 2
        while bit < self.dp:
            steps.append((lambda d, t, s, bit=bit: (d ^ bit, t, s), (d // bit) % 2))
            bit *= 2
        return steps


def to_sibling(d, t, s):
    return (d ^ 1, t, s) if d % 2 == t else None


def swap_core(d, t, s):
    return (d ^ 1, t, s)


def over_home(d, t, s):
    return (d, 1 - t, s) if d % 2 == t else None


def over_away(d, t, s):
    return (d, 1 - t, s) if d % 2 != t else None


def gather_slices(grid, piece, where_from=None):
    current = piece
    for partner, bit in grid.levels():
        def target(d, t, s, partner=partner):
            if where_from is not None and not where_from(d, t):
                return None
            return partner(d, t, s)
        received = grid.send(current, target)
        current = jnp.where(
            bit == 1, jnp.concatenate([received, current]), jnp.concatenate([current, received])
        )
    return current


def reduce_gather(grid, grads, mine, core, slice_index):
    current = grads
    for partner, bit in reversed(grid.levels()):
        half = current.shape[0] // 2
        given = lax.dynamic_slice_in_dim(current, (1 - bit) * half, half).astype(BF16)
        kept = lax.dynamic_slice_in_dim(current, bit * half, half)
        current = kept + grid.send(given, partner).astype(F32)
    away = grid.send(current.astype(BF16), over_away)
    total = (current + away.astype(F32)).astype(BF16)
    total = jnp.where(mine, total, grid.send(total, to_sibling))
    half = total.shape[0] // 2
    part = lax.dynamic_slice_in_dim(total, core * half, half)
    part = gather_slices(grid, part)
    other = grid.send(part, swap_core)
    slices = grid.pairs * grid.sp
    a = part.reshape(slices, half, -1)
    b = other.reshape(slices, half, -1)
    whole = jnp.where(core == 0, jnp.concatenate([a, b], 1), jnp.concatenate([b, a], 1))
    return whole.reshape(grads.shape).astype(F32)


def layer_norm(inputs, scales, shifts):
    row_mean = jnp.mean(inputs, axis=-1, keepdims=True)
    centred = inputs - row_mean
    variance = jnp.mean(centred * centred, axis=-1, keepdims=True)
    return centred * lax.rsqrt(variance + EPSILON) * scales + shifts


def exact_gelu(inputs):
    return jax.nn.gelu(inputs, approximate=False)


def mm(left, right, dims):
    return lax.dot_general(left, right, (dims, ((), ())), preferred_element_type=F32)


def attend(queries, key_rows, values):
    scores = jnp.einsum("qhd,khd->hqk", queries, key_rows, preferred_element_type=F32)
    row_max = jnp.max(scores, axis=-1, keepdims=True)
    weights = jnp.exp(scores - row_max)
    row_total = jnp.sum(weights, axis=-1, keepdims=True)
    weights = weights / row_total
    mixed = jnp.einsum("hqk,khd->qhd", weights.astype(BF16), values, preferred_element_type=F32)
    return mixed, (row_max + jnp.log(row_total))[..., 0]


def attend_back(queries, key_rows, values, log_total, grad_mixed):
    scores = jnp.einsum("qhd,khd->hqk", queries, key_rows, preferred_element_type=F32)
    weights = jnp.exp(scores - log_total[..., None])
    grad_weights = jnp.einsum("qhd,khd->hqk", grad_mixed, values, preferred_element_type=F32)
    inner_sum = jnp.sum(grad_weights * weights, axis=-1, keepdims=True)
    grad_scores = (weights * (grad_weights - inner_sum)).astype(BF16)
    grad_queries = jnp.einsum("hqk,khd->qhd", grad_scores, key_rows, preferred_element_type=F32)
    grad_keys = jnp.einsum("hqk,qhd->khd", grad_scores, queries, preferred_element_type=F32)
    grad_values = jnp.einsum(
        "hqk,qhd->khd", weights.astype(BF16), grad_mixed, preferred_element_type=F32
    )
    return grad_queries, grad_keys, grad_values


def on_device(
    grid,
    frames,
    languages,
    present,
    lang_table,
    norm1_gain,
    norm1_shift,
    qkv_weight,
    qkv_bias,
    out_weight,
    out_bias,
    norm2_gain,
    norm2_shift,
    up_weight,
    up_bias,
    down_weight,
    down_bias,
    grad_out,
):
    d, t, s = (lax.axis_index(name) for name in AXES)
    core = d % 2
    pair = d // 2
    mine = core == t
    slices = grid.pairs * grid.sp
    slice_index = pair * grid.sp + s
    clip = 2 * pair + t
    _, rows, width = frames.shape
    head_width = qkv_weight.shape[2]
    heads = head_width // HEAD
    hidden = up_weight.shape[1]
    langs = lang_table.shape[0]

    def for_clip(value):
        return jnp.where(mine, value, grid.send(value, to_sibling))

    own_frames = for_clip(frames[0])
    across = grid.send(frames[0], lambda d, t, s: (d, t, 1 - s) if d % 2 == t else None)
    other_frames = for_clip(across)
    grad_rows_low = for_clip(grad_out[0])
    numbers = for_clip(jnp.concatenate([languages, present]))
    language, keep = numbers[0], numbers[1].astype(F32)

    def away_group(d, t):
        return d % 2 != t

    def weights_for(parts):
        columns = parts[0].shape[1]
        local = jnp.concatenate(parts) if len(parts) > 1 else parts[0]
        step = local.shape[0] // slices
        piece = lax.dynamic_slice_in_dim(local, slice_index * step, step)
        piece = grid.send(piece, over_home)
        full = gather_slices(grid, piece, away_group)
        full = jnp.where(mine, local, full)
        out, at = [], 0
        for part in parts:
            out.append(lax.slice_in_dim(full, at, at + part.shape[0]))
            at += part.shape[0]
        return out

    qkv_w = weights_for([qkv_weight.reshape(3 * width, head_width)])[0].reshape(3, width, head_width)
    up_l, up_r, down_w, out_w = weights_for(
        [up_weight[:, :width], up_weight[:, width:], down_weight, out_weight]
    )
    up_w = jnp.concatenate([up_l, up_r], axis=1)
    biases = jnp.concatenate([qkv_bias.reshape(-1), up_bias])
    biases = jnp.where(mine, biases, grid.send(biases, over_home)).astype(F32)
    query_bias, value_bias = biases[:head_width], biases[head_width : 2 * head_width]
    up_b = biases[2 * head_width :]

    one_hot = (language == lax.broadcasted_iota(jnp.int32, (1, langs), 1)).astype(F32)
    embedding = jnp.dot(one_hot, lang_table.astype(F32), precision=lax.Precision.HIGHEST)
    gain_one, shift_one = norm1_gain.astype(F32), norm1_shift.astype(F32)
    gain_two, shift_two = norm2_gain.astype(F32), norm2_shift.astype(F32)

    stream = own_frames.astype(F32) + embedding
    normed1, norm1_back = jax.vjp(layer_norm, stream, gain_one, shift_one)
    normed1 = normed1.astype(BF16)
    other_normed = layer_norm(other_frames.astype(F32) + embedding, gain_one, shift_one).astype(BF16)
    both = jnp.concatenate([normed1, other_normed])
    queries = ((mm(normed1, qkv_w[0], ((1,), (0,))) + query_bias) * QUERY_SCALE).astype(BF16)
    key_rows = mm(both, qkv_w[1], ((1,), (0,))).astype(BF16)
    values = (mm(both, qkv_w[2], ((1,), (0,))) + value_bias).astype(BF16)

    query_heads = queries.reshape(rows, heads, HEAD)
    key_heads = key_rows.reshape(-1, heads, HEAD)
    value_heads = values.reshape(-1, heads, HEAD)
    mixed_heads, log_total = attend(query_heads, key_heads, value_heads)
    mixed = mixed_heads.reshape(rows, head_width).astype(BF16)

    def both_cores(part):
        return part + grid.send(part, swap_core)

    attention = both_cores(mm(mixed, out_w, ((1,), (0,))))
    hidden1 = stream + attention + out_bias.astype(F32)
    normed2, norm2_back = jax.vjp(layer_norm, hidden1, gain_two, shift_two)
    normed2 = normed2.astype(BF16)
    pre_act = mm(normed2, up_w, ((1,), (0,))) + up_b
    activation, gelu_back = jax.vjp(exact_gelu, pre_act)
    activation = activation.astype(BF16)
    feed = both_cores(mm(activation, down_w, ((1,), (0,))))
    output = (keep * (hidden1 + feed + down_bias.astype(F32))).astype(BF16)

    grad_rows = keep * grad_rows_low.astype(F32)
    grad_low = grad_rows.astype(BF16)
    grad_activation = mm(grad_low, down_w, ((1,), (1,)))
    grad_pre = gelu_back(grad_activation)[0].astype(BF16)
    grad_normed2 = both_cores(mm(grad_pre, up_w, ((1,), (1,))))
    grad_hidden_norm, grad_norm2_gain, grad_norm2_shift = norm2_back(grad_normed2)
    grad_hidden1 = grad_rows + grad_hidden_norm
    grad_attn_low = grad_hidden1.astype(BF16)
    grad_mixed = mm(grad_attn_low, out_w, ((1,), (1,))).astype(BF16)

    grad_down = mm(activation, grad_low, ((0,), (0,)))
    grad_up = mm(normed2, grad_pre, ((0,), (0,)))
    grad_outw = mm(mixed, grad_attn_low, ((0,), (0,)))
    early = jnp.concatenate([grad_up[:, :width], grad_up[:, width:], grad_down, grad_outw])
    early = reduce_gather(grid, early, mine, core, slice_index)

    grad_query_heads, grad_key_heads, grad_value_heads = attend_back(
        query_heads, key_heads, value_heads, log_total, grad_mixed.reshape(rows, heads, HEAD)
    )
    grad_kv = jnp.stack(
        [grad_key_heads.reshape(-1, head_width), grad_value_heads.reshape(-1, head_width)]
    )
    grad_kv_other = grid.send(grad_kv[:, rows:].astype(BF16), lambda d, t, s: (d, t, 1 - s))
    grad_kv_low = (grad_kv[:, :rows] + grad_kv_other.astype(F32)).astype(BF16)
    grad_query_low = grad_query_heads.reshape(rows, head_width).astype(BF16)
    grad_query_pre = (grad_query_low.astype(F32) * QUERY_SCALE).astype(BF16)
    stacked = jnp.concatenate([grad_query_pre[None], grad_kv_low])
    grad_qkv = jnp.einsum("fd,jfe->jde", normed1, stacked, preferred_element_type=F32)
    late = reduce_gather(grid, grad_qkv.reshape(3 * width, head_width), mine, core, slice_index)
    grad_normed1 = both_cores(
        jnp.einsum("jfe,jde->fd", stacked, qkv_w, preferred_element_type=F32)
    )
    grad_stream_norm, grad_norm1_gain, grad_norm1_shift = norm1_back(grad_normed1)
    grad_stream = grad_hidden1 + grad_stream_norm
    grad_frames = grad_stream.astype(BF16)

    def to_place(value):
        return jnp.where(mine, value, grid.send(value, over_home))

    output = to_place(output)
    grad_frames = to_place(grad_frames)

    clips = grid.dp
    clip_hot = (clip == lax.broadcasted_iota(jnp.int32, (clips, 1), 0)).astype(F32)
    lang_rows = clip_hot * jnp.sum(grad_stream, axis=0, keepdims=True)
    once = jnp.where(s == 0, 1.0, 0.0)
    lang_ids = jnp.broadcast_to(clip_hot * language.astype(F32) * once, (clips, width))
    query_sum = jnp.sum(grad_query_pre.astype(F32), axis=0)
    value_sum = jnp.sum(grad_kv_low[1].astype(F32), axis=0)
    pack = jnp.concatenate(
        [
            lang_rows,
            lang_ids,
            jnp.stack(
                [
                    grad_norm1_gain,
                    grad_norm1_shift,
                    jnp.sum(grad_hidden1, axis=0),
                    grad_norm2_gain,
                    grad_norm2_shift,
                    jnp.sum(grad_rows, axis=0),
                    jnp.concatenate([query_sum, value_sum]),
                ]
            ),
            jnp.sum(grad_pre.astype(F32), axis=0).reshape(-1, width),
        ]
    )
    for partner, _ in grid.levels():
        pack = pack + grid.send(pack, partner)
    pack = pack + grid.send(pack, lambda d, t, s: (d, 1 - t, s))
    halves = pack[2 * clips + 6 :]
    halves = jnp.where(mine, halves, grid.send(halves, to_sibling))
    ids = pack[clips : 2 * clips, :1]
    hot = (ids == lax.broadcasted_iota(jnp.int32, (1, langs), 1).astype(F32)).astype(F32)
    grad_lang_table = lax.dot_general(
        hot, pack[:clips], (((0,), (0,)), ((), ())), precision=lax.Precision.HIGHEST
    )
    v = pack[2 * clips :]
    return (
        output[None],
        grad_frames[None],
        grad_lang_table,
        v[0],
        v[1],
        late.reshape(3, width, head_width),
        halves[0].reshape(2, head_width),
        early[2 * width + hidden :],
        v[2],
        v[3],
        v[4],
        jnp.concatenate([early[:width], early[width : 2 * width]], axis=1),
        halves[1:].reshape(-1),
        early[2 * width : 2 * width + hidden],
        v[5],
    )


def solution(mesh):
    grid = Grid(mesh)
    placed = (
        P("dp", "seq", None),
        P("dp"),
        P("dp"),
        P(),
        P(),
        P(),
        P(None, None, "tensor"),
        P(None, "tensor"),
        P("tensor", None),
        P(),
        P(),
        P(),
        P(None, "tensor"),
        P("tensor"),
        P("tensor", None),
        P(),
        P("dp", "seq", None),
    )
    return jax.shard_map(
        lambda *arrays: on_device(grid, *arrays),
        mesh=mesh,
        in_specs=placed,
        out_specs=(
            P("dp", "seq", None),
            P("dp", "seq", None),
            P(),
            P(),
            P(),
            P(None, None, "tensor"),
            P(None, "tensor"),
            P("tensor", None),
            P(),
            P(),
            P(),
            P(None, "tensor"),
            P("tensor"),
            P("tensor", None),
            P(),
        ),
        check_vma=False,
    )
```

time: 2160 us -> 520 us (0.24)
  waiting for transfers between devices: 983 us -> 86.4 us
  blocking collectives: 886 us -> 0 us
  starting transfers between devices: 1.16 us -> 122 us
  other arithmetic: 58.2 us -> 115 us
    psum x5 -> x0, waiting for transfers between devices: 948 us -> none  [the longest x1 553 us: on_device(): merged = lax.psum(attention_set + mlp_set, ('dp', 'seq'))]
    unnamed x1 -> x0, blocking collectives: 832 us -> none
    ppermute x0 -> x44, starting transfers between devices: none -> 122 us  [send(): return lax.ppermute(value, AXES, moves)]
    ppermute x0 -> x44, waiting for transfers between devices: none -> 86.4 us  [send(): return lax.ppermute(value, AXES, moves)]
    psum x1 -> x0, blocking collectives: 54.5 us -> none  [on_device(): merged = lax.psum(attention_set + mlp_set, ('dp', 'seq'))]
    all_gather x2 -> x0, waiting for transfers between devices: 34.4 us -> none  [the longest x1 29.6 us: on_device(): lax.all_gather(key_rows, 'seq', axis=1, tiled=True)]
    select_n x0 -> x18, other arithmetic: none -> 27.3 us  [the longest x10 12.1 us: gather_slices(): jnp.where(bit == 1, jnp.concatenate([received, current]), jnp.concatenate...]
    dot_general x18 -> x21, matrix products: 124 us -> 122 us  [the longest x12 44.2 us: mm(): lax.dot_general(left, right, (dims, ((), ())), preferred_element_type=F32)]
  transfers between devices with their start and end apart: 7 -> 44, of which waited for: 7 -> 16; matrix products, arithmetic and copies ran while one was open for 3% -> 44% of each run, Pallas kernels for 0% -> 0%
where the time goes in v1:
time: 520 us; the launch traced here: 514 us
  matrix products  131 us (25%)
  starting transfers between devices  122 us (23%)
  other arithmetic  115 us (22%)
  waiting for transfers between devices  86.4 us (17%)
  local copies, waits for them, and re-layouts  54.3 us (10%)
    ppermute x44, starting transfers between devices, send(): return lax.ppermute(value, AXES, moves)  122 us
    ppermute x44, waiting for transfers between devices, send(): return lax.ppermute(value, AXES, moves)  86.4 us
    dot_general x12, matrix products, mm(): lax.dot_general(left, right, (dims, ((), ())), preferred_element_type=F32)  44.2 us
    convert_element_type x1, other arithmetic, attend_back(): grad_scores = (weights * (grad_weights - inner_sum)).astype(BF16)  22.6 us
    dot_general x1, matrix products, attend_back(): jnp.einsum('qhd,khd->hqk', grad_mixed, values, preferred_element_type=F32)  21.6 us
    dot_general x1, matrix products, attend(): jnp.einsum('hqk,khd->qhd', weights.astype(BF16), values, preferred_elemen...  12.8 us
    dot_general x1, matrix products, attend_back(): jnp.einsum('hqk,qhd->khd', weights.astype(BF16), grad_mixed, preferred_el...  12.2 us
    select_n x10, other arithmetic, gather_slices(): jnp.where(bit == 1, jnp.concatenate([received, current]), jnp.concatenate...  12.1 us
  transfers between devices with their start and end apart: 44, of which 16 were waited for; matrix products, arithmetic and copies ran while one was open for 44% of the time, Pallas kernels for 0%

profile of v1, /device:TPU:0, one launch (start us, length us, event | category | flops | bytes accessed | tf_op | source)
XLA Modules:
  0.0 513.6 jit_solution(1780387076246322784)
XLA Ops:
  28.4 7.5 %collective-permute-done.9 = bf16[432,768]{1,0:T(8,128)(2,1)S(1)} collective-permute-done((bf16[432,768]{1,0:T(8,128)(2,1)S(1)}, bf16[432,768]{1,0:T(8,128)(2,1)S(1)}, u32[]{:S(2)}, u32[]{:S(2)}) %collective-permute-start.9) | collective-permute-done | bytes 663584 | tf_op jit(solution)/shard_map/ppermute | solution.py:27
  37.8 12.9 %collective-permute-start.3 = (bf16[750,768]{1,0:T(8,128)(2,1)S(1)}, bf16[750,768]{1,0:T(8,128)(2,1)S(1)}, u32[]{:S(2)}, u32[]{:S(2)}) collective-permute-start(bf16[750,768]{1,0:T(8,128)(2,1)S(1)} %collective-permute-done.2), channel_id=1, source_target_pairs={{0,4},{1,5},{6,2},{7,3},{8,12},{9,13},{14,10},{15,11},{16,20},{17,... | collective-permute-start | bytes 3456008 | tf_op jit(solution)/shard_map/ppermute | solution.py:27
  70.3 11.2 %fusion.93 = (f32[6,750]{1,0:T(8,128)S(1)}, f32[6,750,1500]{2,1,0:T(8,128)}) fusion(bf16[750,6,64]{0,2,1:T(8,128)(2,1)S(1)} %bitcast.81, bf16[1500,6,64]{0,2,1:T(8,128)(2,1)S(1)} %bitcast.70), kind=kOutput, calls=%fused_computation.204 | convolution fusion | flops 870745472 | bytes 28746000 | tf_op jit(solution)/shard_map/qhd,khd->hqk/dot_general | solution.py:109
  86.1 11.1 %fusion = f32[6,750]{1,0:T(8,128)S(1)} fusion(f32[6,750,1500]{2,1,0:T(8,128)} %get-tuple-element.65, f32[6,750]{1,0:T(8,128)S(1)} %get-tuple-element.64), kind=kLoop, calls=%fused_computation.5 | loop fusion | flops 13495500 | bytes 27036000 | tf_op jit(solution)/shard_map/reduce_sum | solution.py:112
  102.9 12.8 %fusion.42 = bf16[6,64,750]{2,1,0:T(8,128)(2,1)} fusion(bf16[1500,6,64]{0,2,1:T(8,128)(2,1)} %bitcast.76, f32[6,750,1500]{2,1,0:T(8,128)} %get-tuple-element.65, f32[6,750]{1,0:T(8,128)S(1)} %fusion, f32[6,750]{1,0:T(8,128)S(1)} %get-tuple-element.64), kind=kOutput, calls=%fused_computation.105 | convolution fusion | flops 884537984 | bytes 28764000 | tf_op jit(solution)/shard_map/hqk,khd->qhd/dot_general | solution.py:114
  115.7 5.3 %fusion.6 = bf16[3456,768]{1,0:T(8,128)(2,1)S(1)} fusion(bf16[1728,768]{1,0:T(8,128)(2,1)S(1)} %maximum_select_fusion.2, bf16[1728,768]{1,0:T(8,128)(2,1)} %collective-permute-done.12, pred[]{:T(512)S(6)} %eq.83, pred[]{:T(512)S(6)} %eq.80, bf16[384,768]{1,0:T(8,128)(2,1)S(1)} %copy-done.26, bf16[1536,768]{1,0:T(8,128)(2,1)} %param.31, ...), kind=kLoop, calls=%fused_computation.14 | loop fusion | flops 47775744 | bytes 15925250 | tf_op jit(solution)/shard_map/jit(_where)/select_n | solution.py:185
  121.9 20.8 %collective-permute-start.13 = (f32[750,768]{1,0:T(8,128)S(1)}, f32[750,768]{1,0:T(8,128)S(1)}, u32[]{:S(2)}, u32[]{:S(2)}) collective-permute-start(f32[750,768]{1,0:T(8,128)S(1)} %fusion.58), channel_id=1, source_target_pairs={{0,4},{1,5},{2,6},{3,7},{4,0},{5,1},{6,2},{7,3},{8,12},{9,13},{10,... | collective-permute-start | bytes 6912008 | tf_op jit(solution)/shard_map/ppermute | solution.py:27
  150.8 13.0 %multiply_convert_fusion.1 = (bf16[750,1536]{1,0:T(8,128)(2,1)}, f32[750,1536]{1,0:T(8,128)S(1)}, f32[750,1536]{1,0:T(8,128)S(1)}) fusion(f32[1536]{0:T(1024)S(1)} %slice.155, bf16[768,768]{1,0:T(8,128)(2,1)S(1)} %get-tuple-element.51, bf16[768,768]{1,0:T(8,128)(2,1)S(1)} %get-tuple-element.50, f32[750,768]{1,0:T(8,128)S(1)} %get-tuple-element.42, ...), kind=kOutput, calls=%fused_computation.25 | convolution fusion | flops 1853102592 | bytes 16201584 | tf_op jit(solution)/shard_map/dot_general | solution.py:105
  209.0 21.6 %multiply_reduce_fusion = (f32[6,750]{1,0:T(8,128)S(1)}, f32[6,750,1500]{2,1,0:T(8,128)}) fusion(f32[6,750,1500]{2,1,0:T(8,128)} %get-tuple-element.65, f32[6,750]{1,0:T(8,128)S(1)} %log_add_fusion, bf16[750,6,64]{0,2,1:T(8,128)(2,1)S(1)} %bitcast.78, bf16[1500,6,64]{0,2,1:T(8,128)(2,1)} %bitcast.77), kind=kOutput, calls=%fused_computation.1 | convolution fusion | flops 884245504 | bytes 55764000 | tf_op jit(solution)/shard_map/qhd,khd->hqk/dot_general | solution.py:121
  230.6 22.6 %multiply_convert_fusion = bf16[6,750,1500]{2,1,0:T(8,128)(2,1)} fusion(f32[6,750,1500]{2,1,0:T(8,128)} %get-tuple-element.68, f32[6,750,1500]{2,1,0:T(8,128)} %get-tuple-element.65, f32[6,750]{1,0:T(8,128)S(1)} %get-tuple-element.67, f32[6,750]{1,0:T(8,128)S(1)} %log_add_fusion), kind=kLoop, calls=%fused_computation | loop fusion | flops 27000000 | bytes 67536000 | tf_op jit(solution)/shard_map/convert_element_type | solution.py:123
  253.3 9.1 %fusion.94 = f32[6,64,1500]{2,1,0:T(8,128)} fusion(bf16[750,6,64]{0,2,1:T(8,128)(2,1)} %bitcast.82, bf16[6,750,1500]{2,1,0:T(8,128)(2,1)} %multiply_convert_fusion), kind=kOutput, calls=%fused_computation.205 | convolution fusion | flops 864000000 | bytes 16380000 | tf_op jit(solution)/shard_map/hqk,qhd->khd/dot_general | solution.py:125
  265.4 12.2 %fusion.2 = f32[6,64,1500]{2,1,0:T(8,128)} fusion(bf16[750,6,64]{0,2,1:T(8,128)(2,1)S(1)} %bitcast.79, f32[6,750,1500]{2,1,0:T(8,128)} %get-tuple-element.65, f32[6,750]{1,0:T(8,128)S(1)} %log_add_fusion), kind=kOutput, calls=%fused_computation.7 | convolution fusion | flops 877500032 | bytes 29898000 | tf_op jit(solution)/shard_map/hqk,qhd->khd/dot_general | solution.py:126
  295.0 9.1 %convert_reduce_fusion.1 = (f32[6,64]{1,0:T(8,128)S(1)}, bf16[6,64,750]{2,1,0:T(8,128)(2,1)S(1)}) fusion(bf16[1500,6,64]{0,2,1:T(8,128)(2,1)S(1)} %bitcast.71, bf16[6,750,1500]{2,1,0:T(8,128)(2,1)} %multiply_convert_fusion), kind=kOutput, calls=%fused_computation.107 | convolution fusion | flops 865727616 | bytes 15229536 | tf_op jit(solution)/shard_map/hqk,khd->qhd/dot_general | solution.py:124
  305.2 7.1 %collective-permute-done.18 = bf16[2,750,384]{2,0,1:T(2,128)(2,1)} collective-permute-done((bf16[2,750,384]{2,0,1:T(2,128)(2,1)}, bf16[2,750,384]{2,0,1:T(2,128)(2,1)}, u32[]{:S(2)}, u32[]{:S(2)}) %collective-permute-start.18) | collective-permute-done | bytes 1152032 | tf_op jit(solution)/shard_map/ppermute | solution.py:27
  333.5 5.3 %fusion.33 = f32[750,768]{1,0:T(8,128)} fusion(bf16[3,768,384]{2,1,0:T(8,128)(2,1)} %param.23, bf16[3,768,384]{2,1,0:T(8,128)(2,1)} %bitcast.88, pred[]{:T(512)S(6)} %eq.80, bf16[2,750,384]{2,1,0:T(8,128)(2,1)} %copy-done.24, bf16[1,750,384]{2,1,0:T(8,128)(2,1)} %copy.67), kind=kOutput, calls=%fused_computation.92 | convolution fusion | flops 1328852736 | bytes 7570945 | tf_op jit(solution)/shard_map/jfe,jde->fd/dot_general | solution.py:265
  338.7 6.8 %collective-permute-done.37 = bf16[432,768]{1,0:T(8,128)(2,1)S(1)} collective-permute-done((bf16[432,768]{1,0:T(8,128)(2,1)}, bf16[432,768]{1,0:T(8,128)(2,1)S(1)}, u32[]{:S(2)}, u32[]{:S(2)}) %collective-permute-start.37) | collective-permute-done | bytes 663584 | tf_op jit(solution)/shard_map/ppermute | solution.py:27
  347.0 6.8 %collective-permute-done.25 = bf16[1152,384]{1,0:T(8,128)(2,1)} collective-permute-done((bf16[1152,384]{1,0:T(8,128)(2,1)}, bf16[1152,384]{1,0:T(8,128)(2,1)}, u32[]{:S(2)}, u32[]{:S(2)}) %collective-permute-start.25) | collective-permute-done | bytes 884768 | tf_op jit(solution)/shard_map/ppermute | solution.py:27
  357.5 10.4 %collective-permute-done.38 = bf16[432,768]{1,0:T(8,128)(2,1)S(1)} collective-permute-done((bf16[432,768]{1,0:T(8,128)(2,1)S(1)}, bf16[432,768]{1,0:T(8,128)(2,1)S(1)}, u32[]{:S(2)}, u32[]{:S(2)}) %collective-permute-start.38) | collective-permute-done | bytes 663584 | tf_op jit(solution)/shard_map/ppermute | solution.py:27
  410.7 11.8 %collective-permute-start.31 = (bf16[288,384]{1,0:T(8,128)(2,1)S(1)}, bf16[288,384]{1,0:T(8,128)(2,1)S(1)}, u32[]{:S(2)}, u32[]{:S(2)}) collective-permute-start(bf16[288,384]{1,0:T(8,128)(2,1)S(1)} %maximum_select_fusion.13), channel_id=1, source_target_pairs={{0,8},{1,9},{2,10},{3,11},{4,12},{5,13},{6,14},{7,15},{8,0},{9,1},... | collective-permute-start | bytes 663560 | tf_op jit(solution)/shard_map/ppermute | solution.py:27
  427.2 9.4 %collective-permute-done.42 = bf16[864,768]{1,0:T(8,128)(2,1)S(1)} collective-permute-done((bf16[864,768]{1,0:T(8,128)(2,1)S(1)}, bf16[864,768]{1,0:T(8,128)(2,1)S(1)}, u32[]{:S(2)}, u32[]{:S(2)}) %collective-permute-start.42) | collective-permute-done | bytes 1327136 | tf_op jit(solution)/shard_map/ppermute | solution.py:27
  445.5 9.1 %collective-permute-start.22 = (f32[25,768]{1,0:T(8,128)S(1)}, f32[25,768]{1,0:T(8,128)S(1)}, u32[]{:S(2)}, u32[]{:S(2)}) collective-permute-start(f32[25,768]{1,0:T(8,128)S(1)} %add.289), channel_id=1, source_target_pairs={{0,8},{1,9},{2,10},{3,11},{4,12},{5,13},{6,14},{7,15},{8,0},{9,1},... | collective-permute-start | bytes 230408 | tf_op jit(solution)/shard_map/ppermute | solution.py:27
  461.4 7.1 %collective-permute-done.23 = f32[25,768]{1,0:T(8,128)S(1)} collective-permute-done((f32[25,768]{1,0:T(8,128)S(1)}, f32[25,768]{1,0:T(8,128)S(1)}, u32[]{:S(2)}, u32[]{:S(2)}) %collective-permute-start.23) | collective-permute-done | bytes 76832 | tf_op jit(solution)/shard_map/ppermute | solution.py:27
  470.3 9.9 %collective-permute-done.24 = f32[25,768]{1,0:T(8,128)S(1)} collective-permute-done((f32[25,768]{1,0:T(8,128)S(1)}, f32[25,768]{1,0:T(8,128)S(1)}, u32[]{:S(2)}, u32[]{:S(2)}) %collective-permute-start.24) | collective-permute-done | bytes 76832 | tf_op jit(solution)/shard_map/ppermute | solution.py:27
  480.2 12.8 %collective-permute-start.34 = (f32[3,768]{1,0:T(4,128)S(1)}, f32[3,768]{1,0:T(4,128)S(1)}, u32[]{:S(2)}, u32[]{:S(2)}) collective-permute-start(f32[3,768]{1,0:T(4,128)S(1)} %slice.164), channel_id=1, source_target_pairs={{0,4},{1,5},{6,2},{7,3},{8,12},{9,13},{14,10},{15,11},{16,20},{17,... | collective-permute-start | bytes 27656 | tf_op jit(solution)/shard_map/ppermute | solution.py:27
  (326 shorter events, 243.3 us)
Async XLA Ops:
  0.7 50.0 %collective-permute-start.1 = (bf16[750,768]{1,0:T(8,128)(2,1)}, bf16[750,768]{1,0:T(8,128)(2,1)}, u32[]{:S(2)}, u32[]{:S(2)}) collective-permute-start(bf16[750,768]{1,0:T(8,128)(2,1)} %bitcast.90), channel_id=1, source_target_pairs={{0,4},{1,5},{6,2},{7,3},{8,12},{9,13},{14,10},{15,11},{16,20},{17,... | collective-permute-start | bytes 3456008 | tf_op jit(solution)/shard_map/ppermute | solution.py:27
  4.2 33.6 %collective-permute-start.2 = (bf16[750,768]{1,0:T(8,128)(2,1)}, bf16[750,768]{1,0:T(8,128)(2,1)S(1)}, u32[]{:S(2)}, u32[]{:S(2)}) collective-permute-start(bf16[750,768]{1,0:T(8,128)(2,1)} %bitcast.91), channel_id=1, source_target_pairs={{0,1},{1,0},{6,7},{7,6},{8,9},{9,8},{14,15},{15,14},{16,17},{17,16... | collective-permute-start | bytes 3456008 | tf_op jit(solution)/shard_map/ppermute | solution.py:27
  12.9 15.5 %collective-permute-start.8 = (bf16[2304]{0:T(1024)(128)(2,1)S(1)}, bf16[2304]{0:T(1024)(128)(2,1)S(1)}, u32[]{:S(2)}, u32[]{:S(2)}) collective-permute-start(bf16[2304]{0:T(1024)(128)(2,1)S(1)} %dynamic-update-slice.1), channel_id=1, source_target_pairs={{0,2},{1,3},{6,4},{7,5},{8,10},{9,11},{14,12},{15,13},{16,18},{17,... | collective-permute-start | bytes 13832 | tf_op jit(solution)/shard_map/ppermute | solution.py:27
  35.9 16.6 %collective-permute-start.10 = (bf16[432,768]{1,0:T(8,128)(2,1)S(1)}, bf16[432,768]{1,0:T(8,128)(2,1)S(1)}, u32[]{:S(2)}, u32[]{:S(2)}) collective-permute-start(bf16[432,768]{1,0:T(8,128)(2,1)S(1)} %collective-permute-done.9), channel_id=1, source_target_pairs={{2,3},{3,2},{4,5},{5,4},{10,11},{11,10},{12,13},{13,12},{18,19},{1... | collective-permute-start | bytes 1990664 | tf_op jit(solution)/shard_map/ppermute | solution.py:27
  37.0 19.0 %collective-permute-start.7 = (bf16[1152,384]{1,0:T(8,128)(2,1)S(1)}, bf16[1152,384]{1,0:T(8,128)(2,1)S(1)}, u32[]{:S(2)}, u32[]{:S(2)}) collective-permute-start(bf16[1152,384]{1,0:T(8,128)(2,1)S(1)} %maximum_select_fusion.8), channel_id=1, source_target_pairs={{2,18},{3,19},{4,20},{5,21},{10,26},{11,27},{12,28},{13,29},{18,2}... | collective-permute-start | bytes 2654216 | tf_op jit(solution)/shard_map/ppermute | solution.py:27
  37.8 20.5 %collective-permute-start.3 = (bf16[750,768]{1,0:T(8,128)(2,1)S(1)}, bf16[750,768]{1,0:T(8,128)(2,1)S(1)}, u32[]{:S(2)}, u32[]{:S(2)}) collective-permute-start(bf16[750,768]{1,0:T(8,128)(2,1)S(1)} %collective-permute-done.2), channel_id=1, source_target_pairs={{0,4},{1,5},{6,2},{7,3},{8,12},{9,13},{14,10},{15,11},{16,20},{17,... | collective-permute-start | bytes 3456008 | tf_op jit(solution)/shard_map/ppermute | solution.py:27
  54.1 43.1 %collective-permute-start.11 = (bf16[864,768]{1,0:T(8,128)(2,1)}, bf16[864,768]{1,0:T(8,128)(2,1)}, u32[]{:S(2)}, u32[]{:S(2)}) collective-permute-start(bf16[864,768]{1,0:T(8,128)(2,1)} %maximum_select_fusion.6), channel_id=1, source_target_pairs={{2,10},{3,11},{4,12},{5,13},{10,2},{11,3},{12,4},{13,5},{18,26},{1... | collective-permute-start | bytes 3981320 | tf_op jit(solution)/shard_map/ppermute | solution.py:27
  100.2 15.5 %collective-permute-start.12 = (bf16[1728,768]{1,0:T(8,128)(2,1)S(1)}, bf16[1728,768]{1,0:T(8,128)(2,1)}, u32[]{:S(2)}, u32[]{:S(2)}) collective-permute-start(bf16[1728,768]{1,0:T(8,128)(2,1)S(1)} %maximum_select_fusion.2), channel_id=1, source_target_pairs={{2,18},{3,19},{4,20},{5,21},{10,26},{11,27},{12,28},{13,29},{18,2}... | collective-permute-start | bytes 7962632 | tf_op jit(solution)/shard_map/ppermute | solution.py:27
  121.9 27.8 %collective-permute-start.13 = (f32[750,768]{1,0:T(8,128)S(1)}, f32[750,768]{1,0:T(8,128)S(1)}, u32[]{:S(2)}, u32[]{:S(2)}) collective-permute-start(f32[750,768]{1,0:T(8,128)S(1)} %fusion.58), channel_id=1, source_target_pairs={{0,4},{1,5},{2,6},{3,7},{4,0},{5,1},{6,2},{7,3},{8,12},{9,13},{10,... | collective-permute-start | bytes 6912008 | tf_op jit(solution)/shard_map/ppermute | solution.py:27
  207.5 78.7 %collective-permute-start.35 = (bf16[1728,768]{1,0:T(8,128)(2,1)}, bf16[1728,768]{1,0:T(8,128)(2,1)}, u32[]{:S(2)}, u32[]{:S(2)}) collective-permute-start(bf16[1728,768]{1,0:T(8,128)(2,1)} %dynamic-slice_convert_fusion), channel_id=1, source_target_pairs={{0,16},{1,17},{2,18},{3,19},{4,20},{5,21},{6,22},{7,23},{8,24},{9,... | collective-permute-start | bytes 7962632 | tf_op jit(solution)/shard_map/ppermute | solution.py:27
  284.7 27.7 %collective-permute-start.18 = (bf16[2,750,384]{2,0,1:T(2,128)(2,1)}, bf16[2,750,384]{2,0,1:T(2,128)(2,1)}, u32[]{:S(2)}, u32[]{:S(2)}) collective-permute-start(bf16[2,750,384]{2,0,1:T(2,128)(2,1)} %copy.65), channel_id=1, source_target_pairs={{0,1},{1,0},{2,3},{3,2},{4,5},{5,4},{6,7},{7,6},{8,9},{9,8},{10,11... | collective-permute-start | bytes 3456008 | tf_op jit(solution)/shard_map/ppermute | solution.py:27
  293.5 31.2 %collective-permute-start.36 = (bf16[864,768]{1,0:T(8,128)(2,1)}, bf16[864,768]{1,0:T(8,128)(2,1)}, u32[]{:S(2)}, u32[]{:S(2)}) collective-permute-start(bf16[864,768]{1,0:T(8,128)(2,1)} %dynamic-slice_convert_fusion.1), channel_id=1, source_target_pairs={{0,8},{1,9},{2,10},{3,11},{4,12},{5,13},{6,14},{7,15},{8,0},{9,1},... | collective-permute-start | bytes 3981320 | tf_op jit(solution)/shard_map/ppermute | solution.py:27
  329.5 16.0 %collective-permute-start.37 = (bf16[432,768]{1,0:T(8,128)(2,1)}, bf16[432,768]{1,0:T(8,128)(2,1)S(1)}, u32[]{:S(2)}, u32[]{:S(2)}) collective-permute-start(bf16[432,768]{1,0:T(8,128)(2,1)} %dynamic-slice_convert_fusion.3), channel_id=1, source_target_pairs={{0,1},{1,0},{2,3},{3,2},{4,5},{5,4},{6,7},{7,6},{8,9},{9,8},{10,11... | collective-permute-start | bytes 1990664 | tf_op jit(solution)/shard_map/ppermute | solution.py:27
  333.0 20.8 %collective-permute-start.25 = (bf16[1152,384]{1,0:T(8,128)(2,1)}, bf16[1152,384]{1,0:T(8,128)(2,1)}, u32[]{:S(2)}, u32[]{:S(2)}) collective-permute-start(bf16[1152,384]{1,0:T(8,128)(2,1)} %dynamic-slice_convert_fusion.2), channel_id=1, source_target_pairs={{0,16},{1,17},{2,18},{3,19},{4,20},{5,21},{6,22},{7,23},{8,24},{9,... | collective-permute-start | bytes 2654216 | tf_op jit(solution)/shard_map/ppermute | solution.py:27
  338.7 83.7 %collective-permute-start.19 = (f32[750,768]{1,0:T(8,128)}, f32[750,768]{1,0:T(8,128)}, u32[]{:S(2)}, u32[]{:S(2)}) collective-permute-start(f32[750,768]{1,0:T(8,128)} %fusion.33), channel_id=1, source_target_pairs={{0,4},{1,5},{2,6},{3,7},{4,0},{5,1},{6,2},{7,3},{8,12},{9,13},{10,... | collective-permute-start | bytes 6912008 | tf_op jit(solution)/shard_map/ppermute | solution.py:27
  345.7 22.3 %collective-permute-start.38 = (bf16[432,768]{1,0:T(8,128)(2,1)S(1)}, bf16[432,768]{1,0:T(8,128)(2,1)S(1)}, u32[]{:S(2)}, u32[]{:S(2)}) collective-permute-start(bf16[432,768]{1,0:T(8,128)(2,1)S(1)} %fusion.47), channel_id=1, source_target_pairs={{2,0},{3,1},{4,6},{5,7},{10,8},{11,9},{12,14},{13,15},{18,16},{19,... | collective-permute-start | bytes 1990664 | tf_op jit(solution)/shard_map/ppermute | solution.py:27
  356.0 15.1 %collective-permute-start.26 = (bf16[576,384]{1,0:T(8,128)(2,1)}, bf16[576,384]{1,0:T(8,128)(2,1)}, u32[]{:S(2)}, u32[]{:S(2)}) collective-permute-start(bf16[576,384]{1,0:T(8,128)(2,1)} %dynamic-slice_convert_fusion.4), channel_id=1, source_target_pairs={{0,8},{1,9},{2,10},{3,11},{4,12},{5,13},{6,14},{7,15},{8,0},{9,1},... | collective-permute-start | bytes 1327112 | tf_op jit(solution)/shard_map/ppermute | solution.py:27
  389.0 16.2 %collective-permute-start.41 = (bf16[432,768]{1,0:T(8,128)(2,1)}, bf16[432,768]{1,0:T(8,128)(2,1)}, u32[]{:S(2)}, u32[]{:S(2)}) collective-permute-start(bf16[432,768]{1,0:T(8,128)(2,1)} %maximum_select_fusion.10), channel_id=1, source_target_pairs={{0,8},{1,9},{2,10},{3,11},{4,12},{5,13},{6,14},{7,15},{8,0},{9,1},... | collective-permute-start | bytes 1990664 | tf_op jit(solution)/shard_map/ppermute | solution.py:27
  390.5 78.7 %collective-permute-start.15 = (bf16[750,768]{1,0:T(8,128)(2,1)}, bf16[750,768]{1,0:T(8,128)(2,1)}, u32[]{:S(2)}, u32[]{:S(2)}) collective-permute-start(bf16[750,768]{1,0:T(8,128)(2,1)} %get-tuple-element.57), channel_id=1, source_target_pairs={{0,2},{1,3},{6,4},{7,5},{8,10},{9,11},{14,12},{15,13},{16,18},{17,... | collective-permute-start | bytes 3456008 | tf_op jit(solution)/shard_map/ppermute | solution.py:27
  407.3 29.2 %collective-permute-start.42 = (bf16[864,768]{1,0:T(8,128)(2,1)S(1)}, bf16[864,768]{1,0:T(8,128)(2,1)S(1)}, u32[]{:S(2)}, u32[]{:S(2)}) collective-permute-start(bf16[864,768]{1,0:T(8,128)(2,1)S(1)} %maximum_select_fusion.7), channel_id=1, source_target_pairs={{0,16},{1,17},{2,18},{3,19},{4,20},{5,21},{6,22},{7,23},{8,24},{9,... | collective-permute-start | bytes 3981320 | tf_op jit(solution)/shard_map/ppermute | solution.py:27
  410.7 43.9 %collective-permute-start.31 = (bf16[288,384]{1,0:T(8,128)(2,1)S(1)}, bf16[288,384]{1,0:T(8,128)(2,1)S(1)}, u32[]{:S(2)}, u32[]{:S(2)}) collective-permute-start(bf16[288,384]{1,0:T(8,128)(2,1)S(1)} %maximum_select_fusion.13), channel_id=1, source_target_pairs={{0,8},{1,9},{2,10},{3,11},{4,12},{5,13},{6,14},{7,15},{8,0},{9,1},... | collective-permute-start | bytes 663560 | tf_op jit(solution)/shard_map/ppermute | solution.py:27
  438.4 61.9 %collective-permute-start.43 = (bf16[1728,768]{1,0:T(8,128)(2,1)}, bf16[1728,768]{1,0:T(8,128)(2,1)}, u32[]{:S(2)}, u32[]{:S(2)}) collective-permute-start(bf16[1728,768]{1,0:T(8,128)(2,1)} %maximum_select_fusion.3), channel_id=1, source_target_pairs={{0,4},{1,5},{2,6},{3,7},{4,0},{5,1},{6,2},{7,3},{8,12},{9,13},{10,... | collective-permute-start | bytes 7962632 | tf_op jit(solution)/shard_map/ppermute | solution.py:27
  454.8 38.4 %collective-permute-start.32 = (bf16[576,384]{1,0:T(8,128)(2,1)S(1)}, bf16[576,384]{1,0:T(8,128)(2,1)S(1)}, u32[]{:S(2)}, u32[]{:S(2)}) collective-permute-start(bf16[576,384]{1,0:T(8,128)(2,1)S(1)} %maximum_select_fusion.12), channel_id=1, source_target_pairs={{0,16},{1,17},{2,18},{3,19},{4,20},{5,21},{6,22},{7,23},{8,24},{9,... | collective-permute-start | bytes 1327112 | tf_op jit(solution)/shard_map/ppermute | solution.py:27
  457.8 38.8 %collective-permute-start.20 = (bf16[750,768]{1,0:T(8,128)(2,1)}, bf16[750,768]{1,0:T(8,128)(2,1)}, u32[]{:S(2)}, u32[]{:S(2)}) collective-permute-start(bf16[750,768]{1,0:T(8,128)(2,1)} %get-tuple-element.54), channel_id=1, source_target_pairs={{0,2},{1,3},{6,4},{7,5},{8,10},{9,11},{14,12},{15,13},{16,18},{17,... | collective-permute-start | bytes 3456008 | tf_op jit(solution)/shard_map/ppermute | solution.py:27
  (77 other events, 1111.2 us)

commit v2 on v0

v2 whole, which is shorter than its diff:
```python
import functools
import types

import jax
import jax.numpy as jnp
from jax import lax
from jax.experimental import pallas as pl
from jax.experimental.pallas import tpu as pltpu
from jax.sharding import PartitionSpec as P

HEAD = 64
EPSILON = 1e-05
QUERY_SCALE = 0.125
AXES = ("dp", "tensor", "seq")
F32 = jnp.float32
BF16 = jnp.bfloat16
NN = (((1,), (0,)), ((), ()))
NT = (((1,), (1,)), ((), ()))
TN = (((0,), (0,)), ((), ()))
VMEM = pl.BlockSpec(memory_space=pltpu.VMEM)
ANY = pl.BlockSpec(memory_space=pl.ANY)
RS = 3


def dg(left, right, dims):
    return lax.dot_general(left, right, dims, preferred_element_type=F32)


def rows_at(start, size):
    return pl.ds(pl.multiple_of(start, 16), size)


class Place:
    def __init__(self, dp):
        self.d, self.t, self.s = (lax.axis_index(name) for name in AXES)
        self.core = lax.rem(self.d, 2)
        self.home = self.core == self.t
        self.away = jnp.logical_not(self.home)
        self.clip = self.d - self.core + self.t
        self.sibling = (self.d + 1 - 2 * self.core, self.t, self.s)
        self.across = (self.d, 1 - self.t, self.s)
        self.level = [((self.d, self.t, 1 - self.s), self.s)]
        bit = 2
        while bit < dp:
            value = lax.rem(self.d // bit, 2)
            self.level.append(((self.d + bit - 2 * bit * value, self.t, self.s), value))
            bit *= 2
        self.peers = [self.sibling, self.across] + [to for to, _ in self.level]

    def enter(self):
        barrier = pltpu.get_barrier_semaphore()
        for to in self.peers:
            pl.semaphore_signal(barrier, inc=1, device_id=to, device_id_type=pl.DeviceIdType.MESH)
        pl.semaphore_wait(barrier, len(self.peers))

    def order(self, part):
        levels = [self.level[(part + j) % RS] for j in range(RS)]
        return [to for to, _ in levels], [bit for _, bit in levels]


class Wires:
    def __init__(self, send_sems, recv_sems):
        self.send_sems, self.recv_sems, self.used = send_sems, recv_sems, 0

    def copy(self, src, dst, to):
        i = self.used
        self.used += 1
        return pltpu.make_async_remote_copy(
            src_ref=src,
            dst_ref=dst,
            send_sem=self.send_sems.at[i],
            recv_sem=self.recv_sems.at[i],
            device_id=to,
            device_id_type=pl.DeviceIdType.MESH,
        )


class Fetch:
    def __init__(self, place, wires, part, local, result):
        self.to, self.bits = place.order(part)
        self.place, self.wires, self.result = place, wires, result
        self.slice = local.shape[0] // 2**RS
        self.at = self.slice * (4 * self.bits[0] + 2 * self.bits[1] + self.bits[2])
        at = rows_at(self.at, self.slice)
        self.crossing = wires.copy(local.at[at], result.at[at], place.across)

        @pl.when(place.home)
        def _():
            self.crossing.start()

    def widen(self, j):
        size = self.slice * 2 ** (RS - 1 - j)
        ref = self.result.at[rows_at(self.at, size)]
        self.at = self.at - self.bits[j] * size
        return self.wires.copy(ref, ref, self.to[j])

    def arrive(self):
        self.moving = self.widen(RS - 1)

        @pl.when(self.place.home)
        def _():
            self.crossing.wait_send()

        @pl.when(self.place.away)
        def _():
            self.crossing.wait_recv()
            self.moving.start()

    def double(self, j):
        before = self.moving
        if j:
            self.moving = self.widen(j - 1)

        @pl.when(self.place.away)
        def _():
            before.wait()
            if j:
                self.moving.start()


class Reduction:
    def __init__(self, place, wires, part, kept, given, stages, lands, result):
        self.to, self.bits = place.order(part)
        self.extra = place.level[RS:]
        self.place, self.wires, self.kept, self.given = place, wires, kept, given
        self.stages, self.lands, self.result = stages, lands, result
        self.slice = result.shape[0] // 2**RS
        self.low = 0
        self.at = self.bits[0] * 4 * self.slice
        self.forwards = []

    def start(self):
        self.moving = self.wires.copy(self.given, self.lands[0], self.to[0])
        self.moving.start()

    def halve(self, j):
        self.moving.wait()
        half = self.slice * 2 ** (RS - 2 - j)
        if j == RS - 1:
            now = rows_at(self.low, self.slice)
            self.kept[now, :] += self.lands[j][...].astype(F32)
            return
        bit = self.bits[j + 1]
        away, home = (1 - bit) * half, bit * half
        self.stages[j][...] = (
            self.kept[rows_at(self.low + away, half), :]
            + self.lands[j][rows_at(away, half), :].astype(F32)
        ).astype(BF16)
        self.moving = self.wires.copy(self.stages[j], self.lands[j + 1], self.to[j + 1])
        self.moving.start()
        self.kept[rows_at(self.low + home, half), :] += self.lands[j][
            rows_at(home, half), :
        ].astype(F32)
        self.low = self.low + home
        self.at = self.at + home

    def cross(self):
        now = rows_at(self.low, self.slice)
        stage = self.stages[RS - 1]
        for number, (to, _) in enumerate(self.extra):
            land = self.lands[RS + 1 + number]
            stage[...] = self.kept[now, :].astype(BF16)
            copy = self.wires.copy(stage, land, to)
            copy.start()
            copy.wait()
            self.kept[now, :] = stage[...].astype(F32) + land[...].astype(F32)
        self.crossing = self.wires.copy(stage, self.lands[RS], self.place.across)

        @pl.when(self.place.away)
        def _():
            stage[...] = self.kept[now, :].astype(BF16)
            self.crossing.start()

    def spread(self, start, size):
        ref = self.result.at[rows_at(start, size)]
        forward = self.wires.copy(ref, ref, self.place.sibling)
        self.forwards.append(forward)
        return forward

    def widen(self, j):
        ref = self.result.at[rows_at(self.at, self.slice * 2 ** (RS - 1 - j))]
        return self.wires.copy(ref, ref, self.to[j])

    def land(self):
        first = self.spread(self.at, self.slice)
        self.moving = self.widen(RS - 1)

        @pl.when(self.place.home)
        def _():
            self.crossing.wait_recv()
            self.result[rows_at(self.at, self.slice), :] = (
                self.kept[rows_at(self.low, self.slice), :] + self.lands[RS][...].astype(F32)
            ).astype(BF16)
            self.moving.start()
            first.start()

        @pl.when(self.place.away)
        def _():
            self.crossing.wait_send()

    def double(self, j):
        size = self.slice * 2 ** (RS - 1 - j)
        bit = self.bits[j]
        came = self.at + (1 - 2 * bit) * size
        self.at = self.at - bit * size
        before, forward = self.moving, self.spread(came, size)
        if j:
            self.moving = self.widen(j - 1)

        @pl.when(self.place.home)
        def _():
            before.wait()
            if j:
                self.moving.start()
            forward.start()

    def finish(self):
        @pl.when(self.place.home)
        def _():
            for forward in self.forwards:
                forward.wait_send()

        @pl.when(self.place.away)
        def _():
            for forward in self.forwards:
                forward.wait_recv()


def pair_lanes(rows):
    return lax.broadcasted_iota(jnp.int32, (rows, 128), 1)


def one_head(pair, e, extra=None):
    lane = pair_lanes(pair.shape[0])
    own = (lane < HEAD) if e == 0 else (lane >= HEAD)
    kept = jnp.where(own, pair, jnp.zeros_like(pair))
    if extra is not None:
        kept = jnp.where(lane == (HEAD if e == 0 else 0), extra, kept)
    return kept


def masked_keys(key_ref, columns, masked, rows, valid):
    row = lax.broadcasted_iota(jnp.int32, (rows, 128), 0)
    bias = jnp.where(row >= valid, -1e30, 0.0).astype(BF16)
    for e in range(2):
        for part in range(2):
            at = pl.ds(part * rows, rows)
            masked[e, at, :] = one_head(key_ref[at, columns], e, bias)


def centre(inputs):
    centred = inputs - jnp.mean(inputs, axis=1, keepdims=True)
    scale = lax.rsqrt(jnp.mean(centred * centred, axis=1, keepdims=True) + EPSILON)
    return centred * scale, scale


def call(kernel, name, collective, ins, outs, scratch, hbm, cost):
    names = list(ins) + list(outs) + list(scratch)

    def body(*refs):
        named = dict(zip(names, refs))
        plain = {name: ref for name, ref in named.items() if isinstance(name, str)}
        kernel(types.SimpleNamespace(table=named, **plain))

    results = pl.pallas_call(
        body,
        out_shape=[jax.ShapeDtypeStruct(*item) for item in outs.values()],
        in_specs=[ANY if item in hbm else VMEM for item in ins],
        out_specs=[ANY if item in hbm else VMEM for item in outs],
        scratch_shapes=list(scratch.values()),
        compiler_params=pltpu.CompilerParams(
            collective_id=collective, has_side_effects=True, vmem_limit_bytes=60 * 2**20
        ),
        cost_estimate=cost,
        name=name,
    )(*ins.values())
    return types.SimpleNamespace(**dict(zip(outs, results)))


def forward_kernel(dp, valid, r):
    place = Place(dp)
    place.enter()
    wires = Wires(r.send_sems, r.recv_sems)
    rows, wide = r.frames.shape
    width = r.query.shape[1]
    home, away = place.home, place.away
    chunk = rows // 3

    first = [Fetch(place, wires, j, r.qkv_local.at[j], r.qkv.at[j]) for j in range(3)]
    info = wires.copy(r.info_local, r.info, place.sibling)
    bias = wires.copy(r.bias_local, r.bias, place.across)
    own = wires.copy(r.frames, r.own, place.sibling)
    beside, onward = [], []
    for c in range(3):
        at = pl.ds(c * chunk, chunk)
        beside.append(wires.copy(r.frames.at[at], r.other.at[at], place.level[0][0]))
        onward.append(wires.copy(r.other.at[at], r.other.at[at], place.sibling))
    grads = wires.copy(r.grad_local, r.grad_rows, place.sibling)
    keep = [
        pltpu.make_async_copy(src, dst, r.local_sems.at[i])
        for i, (src, dst) in enumerate(
            (
                (r.qkv_local, r.qkv),
                (r.grad_local, r.grad_rows),
                (r.up_local, r.up),
                (r.down_local, r.down),
                (r.out_local, r.out),
            )
        )
    ]
    lend = pltpu.make_async_copy(r.out_local, r.out_other, r.local_sems.at[len(keep)])
    lent = wires.copy(r.out, r.out_other, place.sibling)

    @pl.when(home)
    def _():
        info.start()
        bias.start()
        own.start()
        for copy in beside:
            copy.start()
        for copy in keep:
            copy.start()
        r.info[...] = r.info_local[...]
        r.bias[...] = r.bias_local[...]
        r.own[...] = r.frames[...]

    @pl.when(away)
    def _():
        lend.start()

    later = []
    for part in range(RS):
        for local, result in ((r.down_local, r.down), (r.up_local, r.up), (r.out_local, r.out)):
            size = local.shape[0] // RS
            at = pl.ds(part * size, size)
            later.append(Fetch(place, wires, part, local.at[at], result.at[at]))

    @pl.when(home)
    def _():
        grads.start()

    for item in first:
        item.arrive()

    @pl.when(away)
    def _():
        info.wait_recv()
        own.wait_recv()
        bias.wait_recv()

    embedding = r.info[0:1, :]

    def norm(source, c, to):
        normal, _ = centre(source[pl.ds(c * chunk, chunk), :].astype(F32) + embedding)
        normed = normal * r.gain[...] + r.shift[...]
        r.normed[pl.ds(to + c * chunk, chunk), :] = normed.astype(BF16)
        return normed

    for c in range(3):
        r.normed_t[:, c * chunk : (c + 1) * chunk] = norm(r.own, c, 0).T.astype(BF16)
        if c == 0:
            for item in first:
                item.double(2)

        @pl.when(home)
        def _():
            beside[c].wait()
            onward[c].start()

    for item in first:
        item.double(1)
    for c in range(3):

        @pl.when(away)
        def _():
            onward[c].wait_recv()

        norm(r.other, c, rows)
    for item in first:
        item.double(0)

    @pl.when(home)
    def _():
        keep[0].wait()

    r.query[...] = (
        (dg(r.normed[:rows, :], r.qkv[0], NN) + r.bias[0:1, :width]) * QUERY_SCALE
    ).astype(BF16)
    for part in range(2):
        at = pl.ds(part * rows, rows)
        r.key[at, :] = dg(r.normed[at, :], r.qkv[1], NN).astype(BF16)
        r.value[at, :] = (dg(r.normed[at, :], r.qkv[2], NN) + r.bias[0:1, width:]).astype(BF16)
    for item in later:
        item.arrive()

    block = 256
    mixed_copies = []

    def one_pair(p):
        columns = pl.ds(p * 128, 128)
        masked_keys(r.key, columns, r.masked, rows, valid)
        for j in range(3):
            r.qkv_pairs[p, :, j * 128 : (j + 1) * 128] = r.qkv[j, :, columns]

        def one_block(i, _):
            at = pl.ds(pl.multiple_of(i * block, block), block)
            parts, rests = [], []
            for e in range(2):
                queries = one_head(r.query[at, columns], e, jnp.ones((), BF16))
                scores = dg(queries, r.masked[e], NT)
                top = jnp.max(scores, axis=1, keepdims=True)
                weights = jnp.exp(scores - top)
                total = jnp.sum(weights, axis=1, keepdims=True)
                weights = weights * (1.0 / total)
                low = weights.astype(BF16)
                rest = (weights - low.astype(F32)).astype(BF16)
                parts.append(dg(low, r.value[:, columns], NN))
                rests.append(parts[-1] + dg(rest, r.value[:, columns], NN))
                r.lse[pl.ds(2 * p + e, 1), at] = (top + jnp.log(total)).reshape(1, block)
            first = pair_lanes(block) < HEAD
            r.mixed[at, columns] = jnp.where(first, parts[0], parts[1]).astype(BF16)
            r.exact[at, columns] = jnp.where(first, rests[0], rests[1])
            return 0

        lax.fori_loop(0, rows // block, one_block, 0)
        copy = wires.copy(r.mixed.at[:, columns], r.mixed_other.at[:, columns], place.sibling)
        copy.start()
        mixed_copies.append(copy)

    one_pair(0)
    for item in later:
        item.double(2)
    one_pair(1)
    for item in later:
        item.double(1)
    one_pair(2)
    for item in later:
        item.double(0)

    @pl.when(away)
    def _():
        lend.wait()
        lent.start()
        grads.wait_recv()
        lent.wait_send()

    @pl.when(home)
    def _():
        lent.wait_recv()
        for copy in keep[1:]:
            copy.wait()
        info.wait_send()
        bias.wait_send()
        own.wait_send()
        grads.wait_send()
        for copy in onward:
            copy.wait_send()

    for copy in mixed_copies:
        copy.wait()


DOWN, UP, LATE = range(3)


def backward_kernel(dp, valid, r):
    place = Place(dp)
    place.enter()
    wires = Wires(r.send_sems, r.recv_sems)
    extra = len(place.level) - RS
    rows, width = r.query.shape
    wide = r.normed_t.shape[0]
    home, away = place.home, place.away

    def part_of(kind, part):
        stages = [r.table[0, kind, part, i] for i in range(4 if kind == LATE else 3)]
        lands = [r.table[1, kind, part, i] for i in range(4 + extra)]
        return stages, lands

    out_copy = wires.copy(r.output, r.output_to, place.across)

    keep_in = pltpu.make_async_copy(r.output, r.share_stage, r.local_sem)
    keep_out = pltpu.make_async_copy(r.share_stage, r.output_to, r.local_sem)

    @pl.when(home)
    def _():
        out_copy.start()
        keep_in.start()

    early = []
    for part in range(RS):
        for kind, kept, given, result in (
            (DOWN, r.down_keep, r.down_give, r.down_sum),
            (UP, r.up_keep, r.up_give, r.up_sum),
        ):
            stages, lands = part_of(kind, part)
            early.append(
                Reduction(
                    place,
                    wires,
                    part,
                    kept.at[part],
                    given.at[part],
                    stages,
                    lands,
                    result.at[part],
                )
            )
    for item in early:
        item.start()

    def back_pair(p):
        columns = pl.ds(p * 128, 128)
        masked, scaled, plain, given = r.masked, r.scaled, r.plain, r.given
        masked_keys(r.key, columns, masked, rows, valid)
        grad = r.grad_mixed[:, columns]
        for e in range(2):
            query = r.query[:, columns]
            scaled[e] = one_head(query, e, jnp.ones((), BF16))
            plain[e] = one_head(query, e)
            given[e] = one_head(grad, e)
        block = 384

        def one_block(store, first, i, total):
            at = pl.ds(pl.multiple_of(first + i * block, block), block)
            grad_keys, grad_values = [], []
            for e in range(2):
                scores = dg(masked[e, at, :], scaled[e], NT)
                weights = jnp.exp(scores - r.lse[pl.ds(2 * p + e, 1), :])
                grad_weights = dg(r.value[at, columns], given[e], NT)
                grad_scores = (weights * (grad_weights - r.inner[pl.ds(2 * p + e, 1), :])).astype(BF16)
                grad_values.append(dg(weights.astype(BF16), given[e], NN))
                grad_keys.append(dg(grad_scores, plain[e], NN))
                total = total + dg(one_head(r.key[at, columns], e), grad_scores, TN)
            to = pl.ds(pl.multiple_of(i * block, block), block)
            store[p, to, :128] = (grad_keys[0] + grad_keys[1]).astype(store.dtype)
            store[p, to, 128:] = (grad_values[0] + grad_values[1]).astype(store.dtype)
            return total

        total = jnp.zeros((128, rows), F32)
        for store, first in ((r.kv_own, 0), (r.kv_stage, rows)):
            total = lax.fori_loop(
                0, rows // block, functools.partial(one_block, store, first), total
            )
        low = total.T.astype(BF16)
        r.stacked[p, :, :128] = (low.astype(F32) * QUERY_SCALE).astype(BF16)
        copy = wires.copy(r.kv_stage.at[p], r.kv_land.at[p], place.level[0][0])
        copy.start()
        return copy

    late = []

    def after_pair(p, copy):
        copy.wait()
        r.stacked[p, :, 128:] = (r.kv_own[p] + r.kv_land[p].astype(F32)).astype(BF16)
        stacked = r.stacked[p]
        columns = pl.ds(p * 128, 128)
        total = r.late_total.at[p]
        total[:wide, :] = dg(r.normed_t[...], stacked, NN)
        outer = dg(r.mixed_low[:, columns], r.grad_attn[...], TN)
        total[wide : wide + 128, :] = outer[:, : wide // 2]
        total[wide + 128 :, :] = outer[:, wide // 2 :]
        stages, lands = part_of(LATE, p)
        item = Reduction(place, wires, p, total, stages[0], stages[1:], lands, r.late_sum.at[p])
        half = 4 * item.slice
        stages[0][...] = total[rows_at((1 - item.bits[0]) * half, half), :].astype(BF16)
        item.low = item.bits[0] * half
        item.start()
        late.append(item)
        share = dg(stacked, r.qkv_pairs[p], NT)
        if p == 0:
            r.share[...] = share
        else:
            r.share[...] += share
        sums = jnp.sum(stacked.astype(F32), axis=0, keepdims=True)
        r.bias_row[:, p * 128 : (p + 1) * 128] = sums[:, :128]
        r.bias_row[:, width + p * 128 : width + (p + 1) * 128] = sums[:, 256:]

    copy0 = back_pair(0)

    @pl.when(home)
    def _():
        keep_in.wait()
        keep_out.start()

    copy1 = back_pair(1)
    after_pair(0, copy0)
    for item in early:
        item.halve(0)
    copy2 = back_pair(2)
    after_pair(1, copy1)
    late[0].halve(0)
    for item in early:
        item.halve(1)
    after_pair(2, copy2)

    @pl.when(home)
    def _():
        keep_out.wait()

    r.share_stage[...] = r.share[...].astype(BF16)
    share_copy = wires.copy(r.share_stage, r.share_land, place.sibling)
    share_copy.start()
    hidden_copy = pltpu.make_async_copy(r.grad_hidden, r.share, r.hidden_sem)
    hidden_copy.start()
    for item in early:
        item.halve(2)
        item.cross()
    late[0].halve(1)
    late[1].halve(0)
    share_copy.wait()
    hidden_copy.wait()

    gain = r.gain[...]
    chunk = rows // 3
    grad_gain = grad_shift = grad_stream_sum = jnp.zeros((1, wide), F32)
    frame_copies = []
    for c in range(3):
        at = pl.ds(c * chunk, chunk)
        stream = r.frames[at, :].astype(F32) + r.embedding[...]
        normal, scale = centre(stream)
        grad = r.share_stage[at, :].astype(F32) + r.share_land[at, :].astype(F32)
        grad_shift = grad_shift + jnp.sum(grad, axis=0, keepdims=True)
        grad_gain = grad_gain + jnp.sum(grad * normal, axis=0, keepdims=True)
        grad = grad * gain
        grad = (
            grad
            - jnp.mean(grad, axis=1, keepdims=True)
            - normal * jnp.mean(grad * normal, axis=1, keepdims=True)
        ) * scale + r.share[at, :]
        grad_stream_sum = grad_stream_sum + jnp.sum(grad, axis=0, keepdims=True)
        out = r.grad_frames.at[at]
        frame_copy = wires.copy(out, out, place.across)
        frame_copies.append(frame_copy)

        @pl.when(home)
        def _():
            out[...] = grad.astype(BF16)
            frame_copy.start()

    late[2].halve(0)
    late[0].halve(2)
    late[0].cross()
    late[1].halve(1)

    pack = r.pack
    row = lax.broadcasted_iota(jnp.int32, (dp, wide), 0)
    pack[:dp, :] = jnp.where(row == place.clip, grad_stream_sum, 0.0)
    pack[dp:, :] = r.pack_in[...]
    row = lax.broadcasted_iota(jnp.int32, (8, wide), 0)
    pack[dp : dp + 8, :] += (
        jnp.where(row == 0, grad_gain, 0.0)
        + jnp.where(row == 1, grad_shift, 0.0)
        + jnp.where(row == 6, r.bias_row[...], 0.0)
    )
    steps = [to for to, _ in place.level] + [place.across]
    pack_copies = []

    def pack_step(i):
        copy = wires.copy(pack.at[i] if False else r.pack_stage, r.pack_land.at[i], steps[i])
        r.pack_stage[...] = pack[...]
        copy.start()
        pack_copies.append(copy)

    def pack_add(i):
        pack_copies[i].wait()
        pack[...] += r.pack_land[i]

    pack_step(0)
    for item in early:
        item.land()
    pack_add(0)
    pack_step(1)
    late[1].halve(2)
    late[1].cross()
    late[2].halve(1)
    late[0].land()
    for item in early:
        item.double(2)
    pack_add(1)
    pack_step(2)
    late[2].halve(2)
    late[2].cross()
    late[1].land()
    late[0].double(2)
    for item in early:
        item.double(1)
    for i in range(2, len(steps)):
        pack_add(i)
        if i + 1 < len(steps):
            pack_step(i + 1)
    tail_copy = wires.copy(pack.at[pl.ds(dp, 16)], r.pack_tail, place.sibling)
    tail_copy.start()
    late[2].land()
    late[1].double(2)
    late[0].double(1)
    late[2].double(2)
    late[1].double(1)
    for item in early:
        item.double(0)
    late[0].double(0)
    late[2].double(1)
    late[1].double(0)
    late[2].double(0)
    tail_copy.wait()

    @pl.when(home)
    def _():
        out_copy.wait_send()
        for copy in frame_copies:
            copy.wait_send()

    @pl.when(away)
    def _():
        out_copy.wait_recv()
        for copy in frame_copies:
            copy.wait_recv()

    for item in early + late:
        item.finish()


def reduction_buffers(scratch, kind, slice_rows, columns, extra):
    stages = [4, 2, 1, 1] if kind == LATE else [2, 1, 1]
    lands = [4, 2, 1, 1] + [1] * extra
    for part in range(RS):
        for side, sizes in enumerate((stages, lands)):
            for i, size in enumerate(sizes):
                scratch[side, kind, part, i] = pltpu.VMEM((size * slice_rows, columns), BF16)


def levels_of(dp):
    levels = 1
    while 2**levels < dp:
        levels += 1
    return levels


def backward(dp, valid, ins):
    rows, width = ins["query"].shape
    wide = ins["normed_t"].shape[0]
    pairs = width // 128
    levels = levels_of(dp)
    extra = levels - RS
    down, up = ins["down_give"].shape, ins["up_give"].shape
    late_rows = wide + 256
    pack_rows = dp + ins["pack_in"].shape[0]
    outs = dict(
        output_to=((rows, wide), BF16),
        grad_frames=((rows, wide), BF16),
        down_sum=((RS, 2 * down[1], down[2]), BF16),
        up_sum=((RS, 2 * up[1], up[2]), BF16),
        late_sum=((pairs, late_rows, 3 * 128), BF16),
        pack=((pack_rows, wide), F32),
        pack_tail=((16, wide), F32),
    )
    wires = 9 * (2 * RS + 2 + RS + extra) + pairs + 1 + 1 + 3 + levels + 1 + 1
    scratch = dict(
        masked=pltpu.VMEM((2, 2 * rows, 128), BF16),
        scaled=pltpu.VMEM((2, rows, 128), BF16),
        plain=pltpu.VMEM((2, rows, 128), BF16),
        given=pltpu.VMEM((2, rows, 128), BF16),
        kv_own=pltpu.VMEM((pairs, rows, 256), F32),
        kv_stage=pltpu.VMEM((pairs, rows, 256), BF16),
        kv_land=pltpu.VMEM((pairs, rows, 256), BF16),
        stacked=pltpu.VMEM((pairs, rows, 384), BF16),
        late_total=pltpu.VMEM((pairs, late_rows, 384), F32),
        share=pltpu.VMEM((rows, wide), F32),
        share_stage=pltpu.VMEM((rows, wide), BF16),
        share_land=pltpu.VMEM((rows, wide), BF16),
        bias_row=pltpu.VMEM((1, 2 * width), F32),
        pack_stage=pltpu.VMEM((pack_rows, wide), F32),
        pack_land=pltpu.VMEM((levels + 1, pack_rows, wide), F32),
        send_sems=pltpu.SemaphoreType.DMA((wires,)),
        recv_sems=pltpu.SemaphoreType.DMA((wires,)),
        local_sem=pltpu.SemaphoreType.DMA,
        hidden_sem=pltpu.SemaphoreType.DMA,
    )
    reduction_buffers(scratch, DOWN, down[1] // 4, down[2], extra)
    reduction_buffers(scratch, UP, up[1] // 4, up[2], extra)
    reduction_buffers(scratch, LATE, late_rows // 8, 384, extra)
    cost = pl.CostEstimate(flops=2 * 10**10, bytes_accessed=10**8, transcendentals=10**7)
    kernel = functools.partial(backward_kernel, dp, valid)
    hbm = ("output", "output_to", "grad_hidden")
    return call(kernel, "backward", 1, ins, outs, scratch, hbm, cost)


def forward(dp, valid, ins):
    rows, wide = ins["frames"].shape
    width = ins["qkv_local"].shape[2]
    hidden = ins["up_local"].shape[1]
    outs = dict(
        own=((rows, wide), BF16),
        grad_rows=((rows, wide), BF16),
        info=((8, wide), F32),
        bias=((8, wide), F32),
        normed_t=((wide, rows), BF16),
        query=((rows, width), BF16),
        key=((2 * rows, width), BF16),
        value=((2 * rows, width), BF16),
        lse=((width // HEAD, rows), F32),
        mixed=((rows, width), BF16),
        mixed_other=((rows, width), BF16),
        exact=((rows, width), F32),
        qkv_pairs=((width // 128, wide, 384), BF16),
        up=((wide, hidden), BF16),
        down=((hidden, wide), BF16),
        out=((width, wide), BF16),
        out_other=((width, wide), BF16),
    )
    wires = 4 * RS * (1 + RS) + 3 + 6 + 1 + 1 + 3
    scratch = dict(
        other=pltpu.VMEM((rows, wide), BF16),
        normed=pltpu.VMEM((2 * rows, wide), BF16),
        qkv=pltpu.VMEM((3, wide, width), BF16),
        masked=pltpu.VMEM((2, 2 * rows, 128), BF16),
        send_sems=pltpu.SemaphoreType.DMA((wires,)),
        recv_sems=pltpu.SemaphoreType.DMA((wires,)),
        local_sems=pltpu.SemaphoreType.DMA((6,)),
    )
    hbm = (
        "qkv_local",
        "grad_local",
        "up_local",
        "down_local",
        "out_local",
    )
    cost = pl.CostEstimate(flops=10**10, bytes_accessed=10**7, transcendentals=10**7)
    kernel = functools.partial(forward_kernel, dp, valid)
    return call(kernel, "forward", 2, ins, outs, scratch, hbm, cost)


def layer_norm(inputs, scales, shifts):
    row_mean = jnp.mean(inputs, axis=-1, keepdims=True)
    centred = inputs - row_mean
    variance = jnp.mean(centred * centred, axis=-1, keepdims=True)
    return centred * lax.rsqrt(variance + EPSILON) * scales + shifts


def exact_gelu(inputs):
    return jax.nn.gelu(inputs, approximate=False)


def on_device(
    sizes,
    frames,
    languages,
    present,
    lang_table,
    norm1_gain,
    norm1_shift,
    qkv_weight,
    qkv_bias,
    out_weight,
    out_bias,
    norm2_gain,
    norm2_shift,
    up_weight,
    up_bias,
    down_weight,
    down_bias,
    grad_out,
):
    d, t, s = (lax.axis_index(name) for name in AXES)
    home = d % 2 == t
    clips = sizes["dp"]
    _, valid, width = frames.shape
    rows = -(-valid // 256) * 256
    head_width = qkv_weight.shape[2]
    hidden = up_weight.shape[1]
    langs = lang_table.shape[0]
    pairs = head_width // 128
    pad = ((0, rows - valid), (0, 0))

    one_hot = (languages[:, None] == lax.broadcasted_iota(jnp.int32, (1, langs), 1)).astype(F32)
    embedding = jnp.dot(one_hot, lang_table.astype(F32), precision=lax.Precision.HIGHEST)
    lane = lax.broadcasted_iota(jnp.int32, (1, width), 1)
    once = jnp.where(s == 0, languages[:, None].astype(F32), 0.0)
    info = jnp.concatenate(
        [
            embedding,
            jnp.broadcast_to(present[:, None].astype(F32), (1, width)),
            jnp.where(lane == d, once, 0.0),
            jnp.zeros((5, width), F32),
        ]
    )
    biases = jnp.concatenate([qkv_bias.reshape(1, width), up_bias.reshape(-1, width)]).astype(F32)
    gain_one, shift_one = norm1_gain.astype(F32)[None], norm1_shift.astype(F32)[None]
    gain_two, shift_two = norm2_gain.astype(F32), norm2_shift.astype(F32)
    f = forward(
        clips,
        valid,
        dict(
            frames=jnp.pad(frames[0], pad),
            grad_local=jnp.pad(grad_out[0], pad),
            info_local=info,
            bias_local=jnp.pad(biases, ((0, 8 - biases.shape[0]), (0, 0))),
            gain=gain_one,
            shift=shift_one,
            qkv_local=qkv_weight,
            up_local=up_weight,
            down_local=down_weight,
            out_local=out_weight,
        ),
    )
    keep = f.info[1, 0]

    moves = []
    group = sizes["tensor"] * sizes["seq"]
    for a in range(sizes["dp"]):
        moves += [(a * group + b, (a ^ 1) * group + b) for b in range(group)]

    def both_cores(part):
        return part + lax.ppermute(part, AXES, moves)

    attention = dg(f.mixed, f.out, NN) + dg(f.mixed_other, f.out_other, NN)
    stream = f.own.astype(F32) + f.info[:1]
    hidden1 = stream + attention + out_bias.astype(F32)
    normed2, norm2_back = jax.vjp(layer_norm, hidden1, gain_two, shift_two)
    normed2 = normed2.astype(BF16)
    pre_act = dg(normed2, f.up, NN) + f.bias[1:3].reshape(-1)
    activation, gelu_back = jax.vjp(exact_gelu, pre_act)
    activation = activation.astype(BF16)
    feed = both_cores(dg(activation, f.down, NN))
    output = (keep * (hidden1 + feed + down_bias.astype(F32))).astype(BF16)

    grad_rows = keep * f.grad_rows.astype(F32)
    grad_low = grad_rows.astype(BF16)
    grad_activation = dg(grad_low, f.down, NT)
    grad_pre = gelu_back(grad_activation)[0].astype(BF16)
    grad_normed2 = both_cores(dg(grad_pre, f.up, NT))
    grad_hidden_norm, grad_norm2_gain, grad_norm2_shift = norm2_back(grad_normed2)
    grad_hidden1 = grad_rows + grad_hidden_norm
    grad_attn_low = grad_hidden1.astype(BF16)
    grad_mixed = lax.optimization_barrier(dg(grad_attn_low, f.out, NT).astype(BF16))
    grad_down = dg(activation, grad_low, TN)
    grad_up = dg(normed2, grad_pre, TN)

    def halves(grads):
        bits = [s, (d // 2) % 2, (d // 4) % 2]
        give, kept = [], []
        for part, bit in zip(grads.reshape(RS, -1, grads.shape[1]), bits):
            half = part.shape[0] // 2
            give.append(lax.dynamic_slice_in_dim(part, (1 - bit) * half, half).astype(BF16))
            kept.append(lax.dynamic_slice_in_dim(part, bit * half, half))
        return jnp.stack(give), jnp.stack(kept)

    down_give, down_keep = halves(grad_down)
    up_give, up_keep = halves(grad_up)
    zero = jnp.zeros((width,), F32)
    vectors = jnp.concatenate(
        [
            jnp.stack(
                [
                    zero,
                    zero,
                    jnp.sum(grad_hidden1, axis=0),
                    grad_norm2_gain,
                    grad_norm2_shift,
                    jnp.sum(grad_rows, axis=0),
                    zero,
                ]
            ),
            jnp.sum(grad_pre.astype(F32), axis=0).reshape(-1, width),
            f.info[2:3],
        ]
    )
    vectors = jnp.pad(vectors, ((0, 16 - vectors.shape[0]), (0, 0)))
    inner = jnp.sum((grad_mixed.astype(F32) * f.exact).reshape(rows, -1, HEAD), axis=2).T
    b = backward(
        clips,
        valid,
        dict(
            query=f.query,
            key=f.key,
            value=f.value,
            lse=f.lse,
            inner=inner,
            mixed_low=f.mixed,
            grad_mixed=grad_mixed,
            grad_attn=grad_attn_low,
            grad_hidden=grad_hidden1,
            frames=f.own,
            embedding=f.info[:1],
            gain=gain_one,
            normed_t=f.normed_t,
            qkv_pairs=f.qkv_pairs,
            output=output,
            down_give=down_give,
            down_keep=down_keep,
            up_give=up_give,
            up_keep=up_keep,
            pack_in=vectors,
        ),
    )
    v = b.pack[clips:]
    tail = jnp.where(home, v, b.pack_tail)
    late = b.late_sum.astype(F32)
    grad_qkv = late[:, :width].reshape(pairs, width, 3, 128).transpose(2, 1, 0, 3)
    grad_outw = jnp.concatenate([late[:, width : width + 128], late[:, width + 128 :]], axis=2)
    ids = v[9, :clips][:, None]
    hot = (ids == lax.broadcasted_iota(jnp.int32, (1, langs), 1).astype(F32)).astype(F32)
    grad_lang_table = lax.dot_general(
        hot, b.pack[:clips], (((0,), (0,)), ((), ())), precision=lax.Precision.HIGHEST
    )
    return (
        b.output_to[None, :valid],
        b.grad_frames[None, :valid],
        grad_lang_table,
        v[0],
        v[1],
        grad_qkv.reshape(3, width, head_width),
        tail[6].reshape(2, head_width),
        grad_outw.reshape(head_width, width),
        v[2],
        v[3],
        v[4],
        b.up_sum.astype(F32).reshape(width, hidden),
        tail[7:9].reshape(-1),
        b.down_sum.astype(F32).reshape(hidden, width),
        v[5],
    )


def solution(mesh):
    rows = P("dp", "seq", None)
    columns, one = P(None, "tensor"), P("dp")
    placed = (
        rows,
        one,
        one,
        P(),
        P(),
        P(),
        P(None, None, "tensor"),
        columns,
        P("tensor", None),
        P(),
        P(),
        P(),
        columns,
        P("tensor"),
        P("tensor", None),
        P(),
        rows,
    )
    out = (
        rows,
        rows,
        P(),
        P(),
        P(),
        P(None, None, "tensor"),
        columns,
        P("tensor", None),
        P(),
        P(),
        P(),
        columns,
        P("tensor"),
        P("tensor", None),
        P(),
    )
    return jax.shard_map(
        functools.partial(on_device, dict(mesh.shape)),
        mesh=mesh,
        in_specs=placed,
        out_specs=out,
        check_vma=False,
    )
```

time: 2160 us -> 370 us (0.17)
  waiting for transfers between devices: 983 us -> 0.01 us
  blocking collectives: 886 us -> 0 us
  Pallas kernels: 0 us -> 242 us
  matrix products: 134 us -> 51.7 us
  other arithmetic: 58.2 us -> 27.2 us
  local copies, waits for them, and re-layouts: 71.8 us -> 41.3 us
    psum x5 -> x0, waiting for transfers between devices: 948 us -> none  [the longest x1 553 us: on_device(): merged = lax.psum(attention_set + mlp_set, ('dp', 'seq'))]
    unnamed x1 -> x0, blocking collectives: 832 us -> none
    pallas_call x0 -> x2, Pallas kernels: none -> 242 us  [call(): pl.pallas_call(body, out_shape=[jax.ShapeDtypeStruct(*item) for item in o...]
    dot_general x19 -> x11, matrix products: 134 us -> 51.7 us  [the longest x9 49.7 us: dg(): return lax.dot_general(left, right, dims, preferred_element_type=F32)]
    psum x1 -> x0, blocking collectives: 54.5 us -> none  [on_device(): merged = lax.psum(attention_set + mlp_set, ('dp', 'seq'))]
    all_gather x2 -> x0, waiting for transfers between devices: 34.4 us -> none  [the longest x1 29.6 us: on_device(): lax.all_gather(key_rows, 'seq', axis=1, tiled=True)]
    convert_element_type x10 -> x6, other arithmetic: 27.2 us -> 0.72 us  [the longest x1 0.59 us: on_device(): lax.broadcasted_iota(jnp.int32, (1, langs), 1).astype(F32)]
    unnamed x123 -> x74, local copies, waits for them, and re-layouts: 30.6 us -> 6.36 us
  transfers between devices with their start and end apart: 7 -> 2, of which waited for: 7 -> 0; matrix products, arithmetic and copies ran while one was open for 3% -> 9% of each run, Pallas kernels for 0% -> 0%
where the time goes in v2:
time: 370 us; the launch traced here: 365 us
  Pallas kernels  242 us (65%)
  matrix products  51.7 us (14%)
  local copies, waits for them, and re-layouts  41.3 us (11%)
  other arithmetic  27.2 us (7%)
    pallas_call x2, Pallas kernels, call(): pl.pallas_call(body, out_shape=[jax.ShapeDtypeStruct(*item) for item in o...  242 us
    dot_general x9, matrix products, dg(): return lax.dot_general(left, right, dims, preferred_element_type=F32)  49.7 us
  transfers between devices with their start and end apart: 2, of which 0 were waited for; matrix products, arithmetic and copies ran while one was open for 9% of the time, Pallas kernels for 0%

profile of v2, /device:TPU:0, one launch (start us, length us, event | category | flops | bytes accessed | tf_op | source)
XLA Modules:
  0.0 365.2 jit_solution(334022698232580751)
XLA Ops:
  0.7 2.4 pad.17.refs_0_
  8.4 75.4 %forward.1 = (bf16[768,768]{1,0:T(8,128)(2,1)}, bf16[768,768]{1,0:T(8,128)(2,1)}, f32[8,768]{1,0:T(8,128)}, f32[8,768]{1,0:T(8,128)}, bf16[768,768]{1,0:T(8,128)...) custom-call(bf16[768,768]{1,0:T(8,128)(2,1)} %pad.17.refs_0_, ...), custom_call_target="tpu_custom_call" | custom-call | flops 10000000000 | bytes 10000000 | tf_op jit(solution)/shard_map/forward/pallas_call | solution.py:265
  86.6 2.0 fusion.45
  91.1 23.4 %multiply_convert_fusion = (bf16[768,1536]{1,0:T(8,128)(2,1)S(1)}, f32[768,1536]{1,0:T(8,128)S(1)}, f32[768,1536]{1,0:T(8,128)S(1)}) fusion(f32[1536]{0:T(1024)S(1)} %add.144, bf16[768,1536]{1,0:T(8,128)(2,1)} %get-tuple-element.50, f32[768,768]{1,0:T(8,128)S(1)} %get-tuple-element.108, f32[768]{0:T(1024)S(1)} %convert_element_type.130, ...), kind=kOutput, calls=%fused_computation.3 | convolution fusion | flops 1892745216 | bytes 16533504 | tf_op jit(solution)/shard_map/dot_general | solution.py:26
  114.5 4.4 %convert_reduce_fusion = (f32[1536]{0:T(1024)S(1)}, bf16[768,1536]{1,0:T(8,128)(2,1)S(1)}) fusion(f32[768,1536]{1,0:T(8,128)S(1)} %get-tuple-element.90, bf16[1536,768]{1,0:T(8,128)(2,1)S(1)} %copy-done.34, bf16[768,768]{1,0:T(8,128)(2,1)S(1)} %copy-done.12, f32[]{:T(128)} %bitcast.8, f32[768,1536]{1,0:T(8,128)S(1)} %get-tuple-element.109, f32[1536]{0:T(1024)S(1)} %add.144), kind=kOutput, calls=%fused_computation.2 | convolution fusion | flops 1833761280 | bytes 15347716 | tf_op jit(solution)/shard_map/dot_general | solution.py:26
  119.0 3.4 fusion.46
  122.5 3.4 fusion.47
  126.3 4.9 %fusion.8 = f32[1536,768]{1,0:T(8,128)} fusion(bf16[768,1536]{1,0:T(8,128)(2,1)S(1)} %get-tuple-element.89, bf16[768,768]{1,0:T(8,128)(2,1)S(1)} %copy-done.12, f32[]{:T(128)} %bitcast.8), kind=kOutput, calls=%fused_computation.40 | convolution fusion | flops 1813708800 | bytes 8257540 | tf_op jit(solution)/shard_map/dot_general | solution.py:26
  131.3 6.3 %fusion.35 = f32[768,1536]{1,0:T(8,128)} fusion(bf16[768,1536]{1,0:T(8,128)(2,1)} %copy-done.33, f32[768,768]{1,0:T(8,128)S(1)} %get-tuple-element.108, f32[768]{0:T(1024)S(1)} %convert_element_type.130, f32[768]{0:T(1024)S(1)} %convert_element_type.129, f32[768]{0:T(1024)S(1)} %fusion.27, f32[768]{0:T(1024)S(1)} %broadcast_multiply_fusion), kind=kOutput, calls=%fused_computation.93 | convolution fusion | flops 1814888448 | bytes 9449472 | tf_op jit(solution)/shard_map/dot_general | solution.py:26
  137.6 2.3 fusion.41
  144.0 1.6 pad_maximum_fusion.refs_16_
  146.8 2.7 fusion.40
  153.1 3.4 multiply_reduce_fusion
  156.5 4.9 %fusion.39 = (f32[768]{0:T(1024)S(1)}, f32[768,768]{1,0:T(8,128)S(1)}, bf16[768,768]{1,0:T(8,128)(2,1)}) fusion(f32[768]{0:T(1024)S(1)} %multiply_multiply_fusion.5, f32[768,768]{1,0:T(8,128)S(1)} %get-tuple-element.108, f32[768]{0:T(1024)S(1)} %broadcast_multiply_fusion, f32[768]{0:T(1024)S(1)} %fusion.27, f32[768,768]{1,0:T(8,128)S(1)} %get-tuple-element.93, ...), kind=kLoop, calls=%fused_computation.96 | loop fusion | flops 7077120 | bytes 12994564 | tf_op jit(solution)/shard_map/transpose(jvp())/reduce_sum | solution.py:835
  161.5 1.7 fusion.37
  170.4 166.3 %backward.1 = (bf16[768,768]{1,0:T(8,128)(2,1)}, bf16[768,768]{1,0:T(8,128)(2,1)}, bf16[3,512,768]{2,1,0:T(8,128)(2,1)}, bf16[3,256,1536]{2,1,0:T(8,128)(2,1)}, ...) custom-call(bf16[768,384]{1,0:T(8,128)(2,1)} %get-tuple-element.39.refs_0_, ...), custom_call_target="tpu_custom_call" | custom-call | flops 20000000000 | bytes 100000000 | tf_op jit(solution)/shard_map/backward/pallas_call | solution.py:265
  337.4 1.7 slice_reduce_fusion.1
  339.2 1.9 slice.94
  345.2 2.9 copy.38
  348.1 2.4 copy.39
  350.5 2.9 copy.40
  354.0 4.6 %bitcast_convert_fusion.1 = f32[768,1536]{1,0:T(8,128)} fusion(bf16[3,256,1536]{2,1,0:T(8,128)(2,1)} %get-tuple-element.61), kind=kLoop, calls=%fused_computation.22 | loop fusion | flops 1179648 | bytes 7077888 | tf_op jit(solution)/shard_map/reshape | solution.py:1018
  359.3 2.7 bitcast_convert_fusion
  362.0 1.9 fusion.22
  (138 shorter events, 32.7 us)
Async XLA Ops:
  0.6 6.3 %copy-start = (bf16[99,768]{1,0:T(8,128)(2,1)S(1)}, bf16[99,768]{1,0:T(8,128)(2,1)}, u32[]{:S(2)}) copy-start(bf16[99,768]{1,0:T(8,128)(2,1)} %param.20) | copy-start | bytes 456196
  0.7 5.1 %copy-start.24 = (bf16[1536]{0:T(1024)(128)(2,1)S(1)}, bf16[1536]{0:T(1024)(128)(2,1)}, u32[]{:S(2)}) copy-start(bf16[1536]{0:T(1024)(128)(2,1)} %param.30) | copy-start | bytes 9220
  0.7 5.1 %copy-start.31 = (bf16[2,384]{1,0:T(2,128)(2,1)S(1)}, bf16[2,384]{1,0:T(2,128)(2,1)}, u32[]{:S(2)}) copy-start(bf16[2,384]{1,0:T(2,128)(2,1)} %param.24) | copy-start | bytes 4612
  0.7 5.1 %copy-start.29 = (bf16[768]{0:T(1024)(128)(2,1)S(1)}, bf16[768]{0:T(1024)(128)(2,1)}, u32[]{:S(2)}) copy-start(bf16[768]{0:T(1024)(128)(2,1)} %param.21) | copy-start | bytes 4612
  0.7 5.7 %copy-start.30 = (bf16[768]{0:T(1024)(128)(2,1)S(1)}, bf16[768]{0:T(1024)(128)(2,1)}, u32[]{:S(2)}) copy-start(bf16[768]{0:T(1024)(128)(2,1)} %param.22) | copy-start | bytes 4612
  8.4 78.2 %copy-start.25 = (bf16[768]{0:T(1024)(128)(2,1)S(1)}, bf16[768]{0:T(1024)(128)(2,1)}, u32[]{:S(2)}) copy-start(bf16[768]{0:T(1024)(128)(2,1)} %param.26) | copy-start | bytes 4612
  83.8 4.7 %copy-start.14 = (bf16[768,768]{1,0:T(8,128)(2,1)S(1)}, bf16[768,768]{1,0:T(8,128)(2,1)}, u32[]{:S(2)}) copy-start(bf16[768,768]{1,0:T(8,128)(2,1)} %get-tuple-element.45.refs_9_) | copy-start | bytes 3538948
  83.9 4.7 %copy-start.20 = (bf16[768,384]{1,0:T(8,128)(2,1)S(1)}, bf16[768,384]{1,0:T(8,128)(2,1)}, u32[]{:S(2)}) copy-start(bf16[768,384]{1,0:T(8,128)(2,1)} %get-tuple-element.48) | copy-start | bytes 1769476
  83.9 4.7 %copy-start.21 = (bf16[384,768]{1,0:T(8,128)(2,1)S(1)}, bf16[384,768]{1,0:T(8,128)(2,1)}, u32[]{:S(2)}) copy-start(bf16[384,768]{1,0:T(8,128)(2,1)} %get-tuple-element.49) | copy-start | bytes 1769476
  91.1 23.4 %copy-start.12 = (bf16[768,768]{1,0:T(8,128)(2,1)S(1)}, bf16[768,768]{1,0:T(8,128)(2,1)}, u32[]{:S(2)}) copy-start(bf16[768,768]{1,0:T(8,128)(2,1)} %get-tuple-element.44) | copy-start | bytes 3538948
  91.1 23.4 %copy-start.34 = (bf16[1536,768]{1,0:T(8,128)(2,1)S(1)}, bf16[1536,768]{1,0:T(8,128)(2,1)}, u32[]{:S(2)}) copy-start(bf16[1536,768]{1,0:T(8,128)(2,1)} %get-tuple-element.52) | copy-start | bytes 7077892
  114.5 4.5 %copy-start.35 = (bf16[768,1536]{1,0:T(8,128)(2,1)S(1)}, bf16[768,1536]{1,0:T(8,128)(2,1)}, u32[]{:S(2)}) copy-start(bf16[768,1536]{1,0:T(8,128)(2,1)} %get-tuple-element.50) | copy-start | bytes 7077892
  119.0 3.4 copy-start.33
  122.4 30.7 %collective-permute-start = (f32[768,768]{1,0:T(8,128)}, f32[768,768]{1,0:T(8,128)}, u32[]{:S(2)}, u32[]{:S(2)}) collective-permute-start(f32[768,768]{1,0:T(8,128)} %fusion.46), channel_id=1, source_target_pairs={{0,4},{1,5},{2,6},{3,7},{4,0},{5,1},{6,2},{7,3},{8,12},{9,13},{10,... | collective-permute-start | bytes 7077896 | tf_op jit(solution)/shard_map/ppermute | solution.py:914
  125.9 30.6 %collective-permute-start.1 = (f32[768,768]{1,0:T(8,128)}, f32[768,768]{1,0:T(8,128)}, u32[]{:S(2)}, u32[]{:S(2)}) collective-permute-start(f32[768,768]{1,0:T(8,128)} %fusion.47), channel_id=1, source_target_pairs={{0,4},{1,5},{2,6},{3,7},{4,0},{5,1},{6,2},{7,3},{8,12},{9,13},{10,... | collective-permute-start | bytes 7077896 | tf_op jit(solution)/shard_map/ppermute | solution.py:914
  131.3 6.3 %copy-start.6 = (f32[1536,768]{1,0:T(8,128)S(1)}, f32[1536,768]{1,0:T(8,128)}, u32[]{:S(2)}) copy-start(f32[1536,768]{1,0:T(8,128)} %fusion.8) | copy-start | bytes 14155780
  156.5 5.0 %copy-start.13 = (bf16[768,768]{1,0:T(8,128)(2,1)S(1)}, bf16[768,768]{1,0:T(8,128)(2,1)}, u32[]{:S(2)}) copy-start(bf16[768,768]{1,0:T(8,128)(2,1)} %get-tuple-element.44) | copy-start | bytes 3538948
  163.2 3.1 copy-start.11
  339.2 3.3 copy-start.22
  339.2 3.3 copy-start.23
  354.0 5.3 %copy-start.7 = (bf16[3,512,768]{2,1,0:T(8,128)(2,1)S(1)}, bf16[3,512,768]{2,1,0:T(8,128)(2,1)}, u32[]{:S(2)}) copy-start(bf16[3,512,768]{2,1,0:T(8,128)(2,1)} %get-tuple-element.62) | copy-start | bytes 7077892
  359.3 4.6 %copy-start.8 = (f32[3,128,384]{2,1,0:T(8,128)S(1)}, f32[3,128,384]{2,1,0:T(8,128)}, u32[]{:S(2)}) copy-start(f32[3,128,384]{2,1,0:T(8,128)} %get-tuple-element.100) | copy-start | bytes 1769476
  359.3 4.6 %copy-start.9 = (f32[3,128,384]{2,1,0:T(8,128)S(1)}, f32[3,128,384]{2,1,0:T(8,128)}, u32[]{:S(2)}) copy-start(f32[3,128,384]{2,1,0:T(8,128)} %get-tuple-element.101) | copy-start | bytes 1769476
  359.3 5.7 %copy-start.1 = (bf16[99,768]{1,0:T(8,128)(2,1)S(1)}, bf16[99,768]{1,0:T(8,128)(2,1)}, u32[]{:S(2)}) copy-start(bf16[99,768]{1,0:T(8,128)(2,1)} %param.20) | copy-start | bytes 456196
  (14 other events, 27.1 us)
